TPU v7x, 256 devices: a whole 4x4x8 slice. The times are simulated.
256 devices in a mesh: row: 8 (over z_hi, core), col: 32 (over x, z_lo, y).
Axes of the slice: x: 4, y: 4, z: 8 (z_hi: 4, z_lo: 2; z = z_hi * 2 + z_lo), core: 2. Of those that a mesh axis runs over, the one named last changes fastest.
Arguments:
- object_field: float32 [2, 2, 4096, 8192], P(None, None, 'row', 'col'), may hold values from -4 to 4
- probe: float32 [2, 256, 256], replicated, may hold values from -4 to 4
- prop_phase: float32 [256, 256], replicated, may hold values from -3.140625 to 3.140625
- slot_count: int32 [8, 32], P('row', 'col'), may hold values from 1 to 4, as said below
- slot_offset: int32 [8, 32, 4, 2], P('row', 'col'), may hold values from 0 to 511, as said below
- intensity: float32 [8, 32, 4, 256, 256], P('row', 'col'), may hold values from 0.2 to 3
Outputs:
- object_grad: float32 [2, 2, 4096, 8192], P(None, None, 'row', 'col')
- probe_grad: float32 [2, 256, 256], replicated
Inputs may be any that keep to these rules, and one draw needn't show every extreme that they name: `slot_count`: each tile owns 1 to 4 live scan positions; in every draw some tile owns 4, and most own one or two. `slot_offset`: row offsets are below 512 and column offsets below 256; every slot's 256 x 256 window lies inside the object, so it reaches at most into the tiles below, to the right and diagonally below right.
All inputs are finite; a program needn't handle non-finite values.
Results may differ from a plain program's by a relative error of at most 0.00015.
Values sent between devices are 32-bit elements; how exact they have to be, the bound alone decides.
No kernel may reach another device: no remote copies, remote signals or barrier semaphores. Data moves between devices by JAX's collectives and lax.ppermute only.
A program may use at most 128 MiB of HBM per device.

v0:
```python
import math

import jax
import jax.numpy as jnp
from jax import lax
from jax.sharding import PartitionSpec as P


def from_behind(value, axis, steps):
    count = lax.axis_size(axis)
    leading, last = (max(0, -steps), min(count, count - steps))
    return lax.ppermute(value, axis, [(source, source + steps) for source in range(leading, last)])


def matmul(left, right):
    return jnp.dot(left, right, precision=lax.Precision.HIGHEST, preferred_element_type=jnp.float32)


def dft_tables(window):
    indices = jnp.arange(window, dtype=jnp.int32)
    product = indices[:, None] * indices[None, :] % window
    angles = 2.0 * math.pi / window * product.astype(jnp.float32)
    factor = 1.0 / math.sqrt(window)
    return (jnp.cos(angles) * factor, -jnp.sin(angles) * factor)


def transform(wave, cos_table, sin_table):
    real_part, imag_part = wave
    left_real = matmul(cos_table, real_part) - matmul(sin_table, imag_part)
    left_imag = matmul(cos_table, imag_part) + matmul(sin_table, real_part)
    return (
        matmul(left_real, cos_table) - matmul(left_imag, sin_table),
        matmul(left_real, sin_table) + matmul(left_imag, cos_table),
    )


def complex_product(first, second):
    return (
        first[0] * second[0] - first[1] * second[1],
        first[0] * second[1] + first[1] * second[0],
    )


def conjugate_product(first, second):
    return (
        first[0] * second[0] + first[1] * second[1],
        first[0] * second[1] - first[1] * second[0],
    )


def position_terms(patch, measured, probe_wave, kernel, cos_table, sin_table):
    slices = patch.shape[0]
    inverse_sin = -sin_table
    layers = [(patch[index, 0], patch[index, 1]) for index in range(slices)]
    incoming = [probe_wave]
    wave = complex_product(probe_wave, layers[0])
    index = 1
    spectrum = complex_product(kernel, transform(wave, cos_table, sin_table))
    arriving = transform(spectrum, cos_table, inverse_sin)
    incoming.append(arriving)
    wave = complex_product(arriving, layers[index])
    far_field = transform(wave, cos_table, sin_table)
    misfit = far_field[0] * far_field[0] + far_field[1] * far_field[1] - measured
    adjoint = transform((misfit * far_field[0], misfit * far_field[1]), cos_table, inverse_sin)
    gradients = [None] * slices
    for index in reversed(range(slices)):
        gradients[index] = conjugate_product(incoming[index], adjoint)
        adjoint = conjugate_product(layers[index], adjoint)
        if index > 0:
            spectrum = conjugate_product(kernel, transform(adjoint, cos_table, sin_table))
            adjoint = transform(spectrum, cos_table, inverse_sin)
    stacked = jnp.stack([jnp.stack(pair) for pair in gradients])
    return (stacked, jnp.stack(adjoint))


def append_below(field, window):
    arriving = from_behind(field[:, :, :window, :], "row", -1)
    return jnp.concatenate([field, arriving], axis=2)


def append_right(field):
    arriving = from_behind(field, "col", -1)
    return jnp.concatenate([field, arriving], axis=3)


def return_right(buffer, tile_cols, window):
    arriving = from_behind(buffer[:, :, :, tile_cols:], "col", 1)
    return buffer[:, :, :, :tile_cols].at[:, :, :, :window].add(arriving)


def return_below(buffer, tile_rows, window):
    arriving = from_behind(buffer[:, :, tile_rows:, :], "row", 1)
    return buffer[:, :, :tile_rows, :].at[:, :, :window, :].add(arriving)


def per_device(object_field, probe, prop_phase, slot_count, slot_offset, intensity):
    window = probe.shape[-1]
    tile_rows = object_field.shape[2]
    tile_cols = object_field.shape[3]
    capacity = intensity.shape[2]
    cos_table, sin_table = dft_tables(window)
    kernel = (jnp.cos(prop_phase), jnp.sin(prop_phase))
    probe_wave = (probe[0], probe[1])
    extended = append_right(append_below(object_field, window))
    offsets = slot_offset[0, 0]
    measured = intensity[0, 0]
    live_count = slot_count[0, 0]

    def cut_patch(offset):
        return lax.dynamic_slice(
            extended, (0, 0, offset[0], offset[1]), (extended.shape[0], 2, window, window)
        )

    patches = jax.vmap(cut_patch)(offsets)
    locate = lambda counter: counter

    def advance(counter, carry):
        grad_buffer, probe_total = carry
        where_index = locate(counter)
        grad_patch, probe_term = position_terms(
            patches[where_index], measured[where_index], probe_wave, kernel, cos_table, sin_table
        )
        grad_buffer = lax.dynamic_update_index_in_dim(grad_buffer, grad_patch, where_index, 0)
        return (grad_buffer, probe_total + probe_term)

    start_carry = (jnp.zeros_like(patches), jnp.zeros((2, window, window), jnp.float32))
    grad_patches, probe_total = lax.fori_loop(jnp.int32(0), live_count, advance, start_carry)

    def deposit(slot, buffer):
        offset = offsets[slot]
        start = (0, 0, offset[0], offset[1])
        current = lax.dynamic_slice(buffer, start, grad_patches.shape[1:])
        return lax.dynamic_update_slice(buffer, current + grad_patches[slot], start)

    accumulated = lax.fori_loop(0, capacity, deposit, jnp.zeros_like(extended))
    object_grad = return_below(return_right(accumulated, tile_cols, window), tile_rows, window)
    probe_grad = lax.psum(probe_total, ("row", "col"))
    return (object_grad, probe_grad)


def solution(mesh):
    return jax.shard_map(
        per_device,
        mesh=mesh,
        in_specs=(
            P(None, None, "row", "col"),
            P(),
            P(),
            P("row", "col"),
            P("row", "col", None, None),
            P("row", "col", None, None, None),
        ),
        out_specs=(P(None, None, "row", "col"), P()),
        check_vma=False,
    )
```

profile of v0, /device:TPU:34, one launch (start us, length us, event | category | flops | bytes accessed | tf_op | source)
XLA Modules:
  0.0 874.9 jit_solution(16844861013835955442)
XLA Ops:
  10.0 3.1 constant_dynamic-update-slice_fusion.1
  14.4 4.5 collective-permute-start.1
  20.2 61.0 %collective-permute-done.1 = f32[2,2,768,256]{3,2,1,0:T(8,128)} collective-permute-done((f32[2,2,768,256]{3,2,1,0:T(8,128)}, f32[2,2,768,256]{3,2,1,0:T(8,128)}, u32[]{:S(2)}, u32[]{:S(2)}) %collective-permute-start.1) | collective-permute-done | bytes 3145760 | tf_op jit(solution)/shard_map/ppermute | solution.py:12
  81.1 6.3 pad_maximum_fusion
  87.5 2.5 broadcast_in_dim.19.clone
  90.0 19.1 %while.33 = (s32[]{:T(128)}, f32[2,2,768,512]{3,2,1,0:T(8,128)}, s32[4,4]{1,0:T(4,128)S(1)}, f32[4,2,2,256,256]{4,3,2,1,0:T(8,128)}, s32[]{:T(128)}) while((s32[]{:T(128)}, f32[2,2,768,512]{3,2,1,0:T(8,128)}, s32[4,4]{1,0:T(4,128)S(1)}, f32[4,2,2,256,256]{4,3,2,1,0:T(8,128)}, s32[]{:T(128)}) %tuple.117), condition=%wide.while_cond.2, body=%wide.while_body.2.sunk | while | flops 2 | bytes 2098301 | solution.py:110
  90.7 4.0 bitcast_dynamic-update-slice_fusion.2
  95.4 4.2 bitcast_dynamic-update-slice_fusion.2
  100.2 4.2 bitcast_dynamic-update-slice_fusion.2
  105.0 4.1 bitcast_dynamic-update-slice_fusion.2
  109.1 2.5 broadcast_in_dim.19
  111.6 82.2 %while.34 = (s32[]{:T(128)}, f32[4,2,2,256,256]{4,3,2,1,0:T(8,128)}, f32[2,256,256]{2,1,0:T(8,128)S(1)}, s32[]{:T(128)}, f32[4,2,2,256,256]{4,3,2,1,0:T(8,128)},...) while((s32[]{:T(128)}, ...), condition=%wide.region_1.2_spmd.clone.clone, body=%wide.region_0.1_spmd.clone.clone.sunk | while | flops 9719119872 | bytes 49283252 | solution.py:127
  115.4 1.5 convolution_subtract_fusion.20
  118.4 1.5 convolution_add_fusion.22
  121.4 1.5 fusion.499
  124.3 2.1 multiply_add_fusion.9
  127.9 1.5 convolution_subtract_fusion.21
  130.9 1.5 convolution_add_fusion.24
  132.4 1.5 fusion.505
  136.8 1.7 multiply_add_fusion.10
  140.0 1.5 convolution_subtract_fusion.23
  142.9 1.5 convolution_add_fusion.25
  148.9 2.6 fusion.510
  153.0 1.5 convolution_subtract_fusion.25
  161.9 2.0 multiply_subtract_fusion.7
  171.3 1.5 fusion.516
  174.2 1.7 multiply_subtract_fusion.8
  177.4 1.5 convolution_subtract_fusion.27
  186.3 1.6 add_bitcast_fusion.4
  193.9 3.5 broadcast_in_dim.18
  197.4 73.8 %while.32 = (s32[]{:T(128)}, f32[2,2,768,512]{3,2,1,0:T(8,128)}, s32[4,2]{0,1:T(2,128)S(1)}, f32[4,2,2,256,256]{4,3,2,1,0:T(8,128)}, s32[]{:T(128)}, /*index=5*/s32[]{:T(128)}, s32[]{:T(128)}, s32[]{:T(128)}) while((s32[]{:T(128)}, f32[2,2,768,512]{3,2,1,0:T(8,128)}, s32[4,2]{0,1:T(2,128)S(1)}, f32[4,2,2,256,256]{4,3,2,1,0:T(8,128)}, ...), condition=%wide.region_3.4_spmd, body=%wide.region_2.3_spmd.sunk | while | flops 262152 | bytes 5243093 | solution.py:135
  201.8 2.1 bitcast_add_fusion.2
  204.0 12.4 %dynamic_update_slice.17 = f32[2,2,768,512]{3,2,1,0:T(8,128)} dynamic-update-slice(f32[2,2,768,512]{3,2,1,0:T(8,128)} %get-tuple-element.777, f32[2,2,256,256]{3,2,1,0:T(8,128)S(1)} %bitcast_add_fusion.2, s32[]{:T(128)} %constant.131.clone.1..sunk, s32[]{:T(128)} %constant.131.clone.1..sunk, s32[]{:T(128)S(6)} %select_n.279, s32[]{:T(128)S(6)} %select_n.280) | dynamic-update-slice | bytes 2097156 | tf_op jit(solution)/shard_map/while/body/eval_jaxpr/dynamic_update_slice | solution.py:133
  220.8 2.1 bitcast_add_fusion.2
  222.9 11.8 %dynamic_update_slice.17 = f32[2,2,768,512]{3,2,1,0:T(8,128)} dynamic-update-slice(f32[2,2,768,512]{3,2,1,0:T(8,128)} %get-tuple-element.777, f32[2,2,256,256]{3,2,1,0:T(8,128)S(1)} %bitcast_add_fusion.2, s32[]{:T(128)} %constant.131.clone.1..sunk, s32[]{:T(128)} %constant.131.clone.1..sunk, s32[]{:T(128)S(6)} %select_n.279, s32[]{:T(128)S(6)} %select_n.280) | dynamic-update-slice | bytes 2097156 | tf_op jit(solution)/shard_map/while/body/eval_jaxpr/dynamic_update_slice | solution.py:133
  239.2 2.1 bitcast_add_fusion.2
  241.3 11.6 %dynamic_update_slice.17 = f32[2,2,768,512]{3,2,1,0:T(8,128)} dynamic-update-slice(f32[2,2,768,512]{3,2,1,0:T(8,128)} %get-tuple-element.777, f32[2,2,256,256]{3,2,1,0:T(8,128)S(1)} %bitcast_add_fusion.2, s32[]{:T(128)} %constant.131.clone.1..sunk, s32[]{:T(128)} %constant.131.clone.1..sunk, s32[]{:T(128)S(6)} %select_n.279, s32[]{:T(128)S(6)} %select_n.280) | dynamic-update-slice | bytes 2097156 | tf_op jit(solution)/shard_map/while/body/eval_jaxpr/dynamic_update_slice | solution.py:133
  257.4 2.1 bitcast_add_fusion.2
  259.5 11.6 %dynamic_update_slice.17 = f32[2,2,768,512]{3,2,1,0:T(8,128)} dynamic-update-slice(f32[2,2,768,512]{3,2,1,0:T(8,128)} %get-tuple-element.777, f32[2,2,256,256]{3,2,1,0:T(8,128)S(1)} %bitcast_add_fusion.2, s32[]{:T(128)} %constant.131.clone.1..sunk, s32[]{:T(128)} %constant.131.clone.1..sunk, s32[]{:T(128)S(6)} %select_n.279, s32[]{:T(128)S(6)} %select_n.280) | dynamic-update-slice | bytes 2097156 | tf_op jit(solution)/shard_map/while/body/eval_jaxpr/dynamic_update_slice | solution.py:133
  271.1 2.2 slice.119
  273.4 2.1 collective-permute-start.2
  275.4 39.8 %collective-permute-done.2 = f32[2,2,768,256]{3,2,1,0:T(8,128)S(1)} collective-permute-done((f32[2,2,768,256]{3,2,1,0:T(8,128)S(1)}, f32[2,2,768,256]{3,2,1,0:T(8,128)S(1)}, u32[]{:S(2)}, u32[]{:S(2)}) %collective-permute-start.2) | collective-permute-done | bytes 3145760 | tf_op jit(solution)/shard_map/ppermute | solution.py:12
  315.8 1.6 copy-done.2
  317.5 94.1 %collective-permute-start.3 = (f32[2,2,256,256]{3,2,1,0:T(8,128)S(1)}, f32[2,2,256,256]{3,2,1,0:T(8,128)S(1)}, u32[]{:S(2)}, u32[]{:S(2)}) collective-permute-start(f32[2,2,256,256]{3,2,1,0:T(8,128)S(1)} %slice.156), channel_id=1, source_target_pairs={{0,32},{32,64},{64,96},{96,128},{128,160},{160,192},{192,224},{1,3... | collective-permute-start | bytes 3145736 | tf_op jit(solution)/shard_map/ppermute | solution.py:12
  411.6 3.0 slice.154
  414.7 2.3 fusion.292
  417.0 448.9 %all-reduce.2.cloned.1.call-done = f32[2,256,256]{2,1,0:T(8,128)} async-done(((f32[2,256,256]{2,1,0:T(8,128)}), f32[2,256,256]{2,1,0:T(8,128)}) %all-reduce.2.cloned.1.call-update) | async-done | bytes 524304 | tf_op jit(solution)/shard_map/psum | solution.py:137
  865.9 1.9 copy.37
  (81 shorter events, 59.7 us)
Async XLA Ops:
  7.2 11.7 %copy-start.5 = (s32[1,1,4,2]{2,3,1,0:T(2,128)S(1)}, s32[1,1,4,2]{2,3,1,0:T(2,128)}, u32[]{:S(2)}) copy-start(s32[1,1,4,2]{2,3,1,0:T(2,128)} %param.20) | copy-start | bytes 100
  7.2 12.0 %copy-start.3 = (f32[2,256,256]{2,1,0:T(8,128)S(1)}, f32[2,256,256]{2,1,0:T(8,128)}, u32[]{:S(2)}) copy-start(f32[2,256,256]{2,1,0:T(8,128)} %param.17) | copy-start | bytes 1572868
  7.2 858.8 %all-reduce.2.cloned.1.call-start = ((), (), s32[]{:S(2)}) async-start(), calls=%async_computation | async-start | bytes 1048576 | tf_op jit(solution)/shard_map/psum | solution.py:137
  8.6 10.6 %copy-start.4 = (f32[256,256]{1,0:T(8,128)S(1)}, f32[256,256]{1,0:T(8,128)}, u32[]{:S(2)}) copy-start(f32[256,256]{1,0:T(8,128)} %param.18) | copy-start | bytes 786436
  8.6 4.7 collective-permute-start
  14.4 66.8 %collective-permute-start.1 = (f32[2,2,768,256]{3,2,1,0:T(8,128)}, f32[2,2,768,256]{3,2,1,0:T(8,128)}, u32[]{:S(2)}, u32[]{:S(2)}) collective-permute-start(f32[2,2,768,256]{3,2,1,0:T(8,128)} %constant_dynamic-update-slice_fusion), channel_id=1, source_target_pairs={{1,0},{2,1},{3,2},{4,3},{5,4},{6,5},{7,6},{8,7},{9,8},{10,9},{11,1... | collective-permute-start | bytes 9437192 | tf_op jit(solution)/shard_map/ppermute | solution.py:12
  193.9 3.5 copy-start.1
  271.1 44.1 %copy-start = (f32[2,2,768,512]{3,2,1,0:T(8,128)S(1)}, f32[2,2,768,512]{3,2,1,0:T(8,128)}, u32[]{:S(2)}) copy-start(f32[2,2,768,512]{3,2,1,0:T(8,128)} %get-tuple-element.367) | copy-start | bytes 18874372
  273.4 41.8 %collective-permute-start.2 = (f32[2,2,768,256]{3,2,1,0:T(8,128)S(1)}, f32[2,2,768,256]{3,2,1,0:T(8,128)S(1)}, u32[]{:S(2)}, u32[]{:S(2)}) collective-permute-start(f32[2,2,768,256]{3,2,1,0:T(8,128)S(1)} %slice.119), channel_id=1, source_target_pairs={{0,1},{1,2},{2,3},{3,4},{4,5},{5,6},{6,7},{7,8},{8,9},{9,10},{10,1... | collective-permute-start | bytes 9437192 | tf_op jit(solution)/shard_map/ppermute | solution.py:12
  315.8 1.6 copy-start.2
  317.5 97.1 %collective-permute-start.3 = (f32[2,2,256,256]{3,2,1,0:T(8,128)S(1)}, f32[2,2,256,256]{3,2,1,0:T(8,128)S(1)}, u32[]{:S(2)}, u32[]{:S(2)}) collective-permute-start(f32[2,2,256,256]{3,2,1,0:T(8,128)S(1)} %slice.156), channel_id=1, source_target_pairs={{0,32},{32,64},{64,96},{96,128},{128,160},{160,192},{192,224},{1,3... | collective-permute-start | bytes 3145736 | tf_op jit(solution)/shard_map/ppermute | solution.py:12
Sparse Core Ops, SparseCore 0:
  411.7 454.1 all-reduce.1
where the time goes:
time: 886 us; the launch traced here: 875 us
  waiting for transfers between devices  550 us (62%)
  starting transfers between devices  102 us (12%)
  local copies, waits for them, and re-layouts  94.5 us (11%)
  matrix products  73.5 us (8%)
  loops' own time  21.3 us (2%)
  other arithmetic  19.2 us (2%)
  between operations  14.4 us (2%)
    psum x1, waiting for transfers between devices, per_device(): probe_grad = lax.psum(probe_total, ('row', 'col'))  449 us
    ppermute x4, starting transfers between devices, from_behind(): lax.ppermute(value, axis, [(source, source + steps) for source in range(l...  102 us
    ppermute x4, waiting for transfers between devices, from_behind(): lax.ppermute(value, axis, [(source, source + steps) for source in range(l...  101 us
    dot_general x48, matrix products, matmul(): jnp.dot(left, right, precision=lax.Precision.HIGHEST, preferred_element_t...  73.5 us
    dynamic_update_slice x4, local copies, waits for them, and re-layouts, deposit(): return lax.dynamic_update_slice(buffer, current + grad_patches[slot], start)  47.4 us
    gather x12, local copies, waits for them, and re-layouts  19.1 us
  transfers between devices with their start and end apart: 5, of which 4 were waited for; matrix products, arithmetic and copies ran while one was open for 1% of the time, Pallas kernels for 0%

commit v1 on v0

v1 whole, which is shorter than its diff:
```python
import math

import jax
import jax.numpy as jnp
import ml_dtypes
import numpy as np
from jax import lax
from jax.experimental import pallas as pl
from jax.experimental.pallas import tpu as pltpu
from jax.sharding import PartitionSpec as P

VMEM = pltpu.VMEM
SMEM = pltpu.SMEM
LIMIT = 40 * 1024 * 1024


def dft_blocks(window):
    indices = np.arange(window)
    angles = 2.0 * math.pi / window * (indices[:, None] * indices[None, :] % window)
    cos, sin = np.cos(angles) / math.sqrt(window), np.sin(angles) / math.sqrt(window)
    ahead = np.block([[cos, -sin], [sin, cos]])
    behind = np.block([[cos, sin], [-sin, cos]])
    parts = []
    for table in (ahead, behind):
        high = table.astype(ml_dtypes.bfloat16)
        low = (table - high.astype(np.float64)).astype(ml_dtypes.bfloat16)
        parts.append(np.stack([high, low]))
    return np.stack(parts)


def halves(value):
    high = value.astype(jnp.bfloat16)
    return high, (value - high.astype(jnp.float32)).astype(jnp.bfloat16)


def dot(left, right):
    return jnp.dot(left, right, preferred_element_type=jnp.float32)


def along_columns(wave, table):
    window = wave[0].shape[0]
    high, low = halves(jnp.concatenate(wave, axis=1))
    out = dot(high, table[0]) + dot(low, table[0]) + dot(high, table[1])
    return out[:, :window], out[:, window:]


def along_rows(wave, table):
    window = wave[0].shape[0]
    high, low = halves(jnp.concatenate(wave, axis=0))
    out = dot(table[0], high) + dot(table[0], low) + dot(table[1], high)
    return out[:window], out[window:]


def forward(wave, tables):
    return along_rows(along_columns(wave, tables.at[0]), tables.at[1])


def inverse(wave, tables):
    return along_rows(along_columns(wave, tables.at[1]), tables.at[0])


def product(first, second):
    return (
        first[0] * second[0] - first[1] * second[1],
        first[0] * second[1] + first[1] * second[0],
    )


def conjugate_product(first, second):
    return (
        first[0] * second[0] + first[1] * second[1],
        first[0] * second[1] - first[1] * second[0],
    )


def corner(offsets, slot, window):
    row, column = offsets[slot, 0], offsets[slot, 1]
    block = row // window
    rows = lax.broadcasted_iota(jnp.int32, (window, window), 0)
    columns = lax.broadcasted_iota(jnp.int32, (window, window), 1)
    row = row - block * window
    return block, row, column, rows >= row, columns >= column


def cut(place, own, right_top, right_bottom, below, diagonal, window):
    block, _, _, upper, left = place
    first = block == 0
    out = []
    for part in range(2):
        own_top, own_bottom = own[part, :window], own[part, window:]
        top = jnp.where(
            left,
            jnp.where(first, own_top, own_bottom),
            jnp.where(first, right_top[part], right_bottom[part]),
        )
        bottom = jnp.where(
            left,
            jnp.where(first, own_bottom, below[part]),
            jnp.where(first, right_bottom[part], diagonal[part]),
        )
        out.append(jnp.where(upper, top, bottom))
    return tuple(out)


def deposit(place, total, term):
    block, _, _, upper, left = place
    for part in range(2):
        value = term[part]
        top = jnp.where(upper, value, 0.0)
        bottom = value - top
        for rows, piece in ((block, top), (block + 1, bottom)):
            kept = jnp.where(left, piece, 0.0)
            total[0, rows, part] += kept
            total[1, rows, part] += piece - kept


def shifted(wave, row, column):
    return tuple(pltpu.roll(pltpu.roll(part, row, 0), column, 1) for part in wave)


def arrive_kernel(
    count, offsets, own, right_top, right_bottom, below, diagonal, probe, kernel, tables, arriving
):
    window = probe.shape[-1]
    slot = pl.program_id(0)

    @pl.when(slot < count[0, 0])
    def _():
        place = corner(offsets, slot, window)
        layer = cut(place, own.at[0], right_top, right_bottom, below, diagonal, window)
        incoming = shifted((probe[0], probe[1]), place[1], place[2])
        spectrum = forward(product(incoming, layer), tables)
        out = inverse(product((kernel[0], kernel[1]), spectrum), tables)
        arriving[0, 0], arriving[0, 1] = out


def misfit_kernel(
    count, offsets, own, right_top, right_bottom, below, diagonal, arriving, measured, tables,
    total, leaving,
):
    window = measured.shape[-1]
    slot = pl.program_id(0)

    @pl.when(slot == 0)
    def _():
        total[...] = jnp.zeros_like(total)

    @pl.when(slot < count[0, 0])
    def _():
        place = corner(offsets, slot, window)
        layer = cut(place, own.at[0], right_top, right_bottom, below, diagonal, window)
        wave = (arriving[0, 0], arriving[0, 1])
        far = forward(product(wave, layer), tables)
        misfit = far[0] * far[0] + far[1] * far[1] - measured[0]
        adjoint = inverse((misfit * far[0], misfit * far[1]), tables)
        deposit(place, total, conjugate_product(wave, adjoint))
        out = conjugate_product(layer, adjoint)
        leaving[0, 0], leaving[0, 1] = out


def leave_kernel(
    count, offsets, own, right_top, right_bottom, below, diagonal, probe, kernel, leaving, tables,
    total, probe_total,
):
    window = probe.shape[-1]
    slot = pl.program_id(0)

    @pl.when(slot == 0)
    def _():
        total[...] = jnp.zeros_like(total)
        probe_total[...] = jnp.zeros_like(probe_total)

    @pl.when(slot < count[0, 0])
    def _():
        place = corner(offsets, slot, window)
        layer = cut(place, own.at[0], right_top, right_bottom, below, diagonal, window)
        incoming = shifted((probe[0], probe[1]), place[1], place[2])
        spectrum = forward((leaving[0, 0], leaving[0, 1]), tables)
        adjoint = inverse(conjugate_product((kernel[0], kernel[1]), spectrum), tables)
        deposit(place, total, conjugate_product(incoming, adjoint))
        term = conjugate_product(layer, adjoint)
        term = shifted(term, (window - place[1]) % window, (window - place[2]) % window)
        probe_total[0] += term[0]
        probe_total[1] += term[1]


def whole(shape):
    return pl.BlockSpec(shape, lambda slot: (0,) * len(shape))


def call(body, capacity, window, layer, operands, specs, outs, out_specs, name):
    block = (2, window, window)
    passes = 2 * 24 * 2 * window**3
    return pl.pallas_call(
        body,
        grid=(capacity,),
        in_specs=[
            pl.BlockSpec(memory_space=SMEM),
            pl.BlockSpec(memory_space=SMEM),
            pl.BlockSpec((1, 2, 2 * window, window), lambda slot: (layer, 0, 0, 0)),
            whole(block),
            whole(block),
            whole(block),
            whole(block),
            *specs,
        ],
        out_shape=outs,
        out_specs=out_specs,
        name=name,
        compiler_params=pltpu.CompilerParams(vmem_limit_bytes=LIMIT),
        cost_estimate=pl.CostEstimate(
            flops=capacity * passes, bytes_accessed=8 * 1024 * 1024, transcendentals=0
        ),
    )(*operands)


def from_behind(value, axis, steps):
    count = lax.axis_size(axis)
    leading, last = (max(0, -steps), min(count, count - steps))
    return lax.ppermute(value, axis, [(source, source + steps) for source in range(leading, last)])


def exchange(value, axis, bit):
    return lax.ppermute(value, axis, [(i, i ^ bit) for i in range(lax.axis_size(axis))])


def sum_everywhere(value):
    shape = value.shape
    value = value.reshape(-1, shape[-1])
    scattered = (("row", 1), ("col", 1), ("col", 8))
    whole_sums = (("col", 2), ("col", 16), ("col", 4), ("row", 2), ("row", 4))
    for axis, bit in scattered:
        first = lax.axis_index(axis) & bit == 0
        low, high = jnp.split(value, 2)
        kept, sent = jnp.where(first, low, high), jnp.where(first, high, low)
        value = kept + exchange(sent, axis, bit)
    for axis, bit in whole_sums:
        value = value + exchange(value, axis, bit)
    for axis, bit in reversed(scattered):
        first = lax.axis_index(axis) & bit == 0
        other = exchange(value, axis, bit)
        value = jnp.concatenate([jnp.where(first, value, other), jnp.where(first, other, value)])
    return value.reshape(shape)


def per_device(object_field, probe, prop_phase, slot_count, slot_offset, intensity):
    window = probe.shape[-1]
    capacity = intensity.shape[2]
    offsets = slot_offset[0, 0]
    measured = intensity[0, 0]
    tables = jnp.asarray(dft_blocks(window))
    kernel = jnp.stack([jnp.cos(prop_phase), jnp.sin(prop_phase)])
    block = (2, window, window)
    f32 = jnp.float32
    per_slot = jax.ShapeDtypeStruct((capacity, *block), f32)
    slot_spec = pl.BlockSpec((1, *block), lambda slot: (slot, 0, 0, 0))
    table_spec = whole(tables.shape)
    total_shape = (2, 3, *block)
    total = jax.ShapeDtypeStruct(total_shape, f32)

    def halo(layer):
        top, bottom = object_field[layer, :, :window], object_field[layer, :, window:]
        right_top = from_behind(top, "col", -1)
        below = from_behind(top, "row", -1)
        right_bottom = from_behind(bottom, "col", -1)
        diagonal = from_behind(right_top, "row", -1)
        return right_top, right_bottom, below, diagonal

    def gather(total):
        own, right = total[0], total[1]
        below = from_behind(own[2], "row", 1)
        diagonal = from_behind(right[2], "row", 1)
        from_left_top = from_behind(right[0] + diagonal, "col", 1)
        from_left_bottom = from_behind(right[1], "col", 1)
        return jnp.concatenate([own[0] + below + from_left_top, own[1] + from_left_bottom], axis=1)

    near = halo(0)
    far = halo(1)
    first = (slot_count, offsets, object_field)
    arriving = call(
        arrive_kernel, capacity, window, 0,
        (*first, *near, probe, kernel, tables),
        (whole(block), whole(block), table_spec),
        per_slot, slot_spec, "arrive",
    )
    last_total, leaving = call(
        misfit_kernel, capacity, window, 1,
        (*first, *far, arriving, measured, tables),
        (slot_spec, pl.BlockSpec((1, window, window), lambda slot: (slot, 0, 0)), table_spec),
        (total, per_slot), (whole(total_shape), slot_spec), "misfit",
    )
    first_total, probe_total = call(
        leave_kernel, capacity, window, 0,
        (*first, *near, probe, kernel, leaving, tables),
        (whole(block), whole(block), slot_spec, table_spec),
        (total, jax.ShapeDtypeStruct(block, f32)), (whole(total_shape), whole(block)), "leave",
    )
    last_grad = gather(last_total)
    first_grad = gather(first_total)
    probe_grad = sum_everywhere(probe_total)
    return (jnp.stack([first_grad, last_grad]), probe_grad)


def solution(mesh):
    return jax.shard_map(
        per_device,
        mesh=mesh,
        in_specs=(
            P(None, None, "row", "col"),
            P(),
            P(),
            P("row", "col"),
            P("row", "col", None, None),
            P("row", "col", None, None, None),
        ),
        out_specs=(P(None, None, "row", "col"), P()),
        check_vma=False,
    )
```

time: 886 us -> 255 us (0.29); the launches traced: 875 us -> 256 us
  waiting for transfers between devices: 550 us -> 108 us
  local copies, waits for them, and re-layouts: 94.5 us -> 8.11 us
  matrix products: 73.5 us -> 0 us
  Pallas kernels: 0 us -> 26.2 us
  loops' own time: 21.3 us -> 0 us
  other arithmetic: 19.2 us -> 5.04 us
  between operations: 14.4 us -> 1.8 us
    psum x1 -> x0, waiting for transfers between devices: 449 us -> none  [per_device(): probe_grad = lax.psum(probe_total, ('row', 'col'))]
    dot_general x48 -> x0, matrix products: 73.5 us -> none  [matmul(): jnp.dot(left, right, precision=lax.Precision.HIGHEST, preferred_element_t...]
    ppermute x0 -> x11, starting transfers between devices: none -> 62.3 us  [exchange(): lax.ppermute(value, axis, [(i, i ^ bit) for i in range(lax.axis_size(axis...]
    ppermute x4 -> x16, starting transfers between devices: 102 us -> 44.2 us  [from_behind(): lax.ppermute(value, axis, [(source, source + steps) for source in range(l...]
    dynamic_update_slice x4 -> x0, local copies, waits for them, and re-layouts: 47.4 us -> none  [deposit(): return lax.dynamic_update_slice(buffer, current + grad_patches[slot], start)]
    ppermute x0 -> x11, waiting for transfers between devices: none -> 28.9 us  [exchange(): lax.ppermute(value, axis, [(i, i ^ bit) for i in range(lax.axis_size(axis...]
    pallas_call x0 -> x3, Pallas kernels: none -> 26.2 us  [call(): pl.pallas_call(body, grid=(capacity,), in_specs=[pl.BlockSpec(memory_spac...]
    ppermute x4 -> x16, waiting for transfers between devices: 101 us -> 79.2 us  [from_behind(): lax.ppermute(value, axis, [(source, source + steps) for source in range(l...]
  transfers between devices with their start and end apart: 5 -> 27, of which waited for: 4 -> 14; matrix products, arithmetic and copies ran while one was open for 1% -> 2% of each run, Pallas kernels for 0% -> 3%
where the time goes in v1:
time: 255 us; the launch traced here: 256 us
  waiting for transfers between devices  108 us (42%)
  starting transfers between devices  106 us (42%)
  Pallas kernels  26.2 us (10%)
  local copies, waits for them, and re-layouts  8.11 us (3%)
  other arithmetic  5.04 us (2%)
    ppermute x16, waiting for transfers between devices, from_behind(): lax.ppermute(value, axis, [(source, source + steps) for source in range(l...  79.2 us
    ppermute x11, starting transfers between devices, exchange(): lax.ppermute(value, axis, [(i, i ^ bit) for i in range(lax.axis_size(axis...  62.3 us
    ppermute x16, starting transfers between devices, from_behind(): lax.ppermute(value, axis, [(source, source + steps) for source in range(l...  44.2 us
    ppermute x11, waiting for transfers between devices, exchange(): lax.ppermute(value, axis, [(i, i ^ bit) for i in range(lax.axis_size(axis...  28.9 us
    pallas_call x3, Pallas kernels, call(): pl.pallas_call(body, grid=(capacity,), in_specs=[pl.BlockSpec(memory_spac...  26.2 us
  transfers between devices with their start and end apart: 27, of which 14 were waited for; matrix products, arithmetic and copies ran while one was open for 2% of the time, Pallas kernels for 3%

profile of v1, /device:TPU:34, one launch (start us, length us, event | category | flops | bytes accessed | tf_op | source)
XLA Modules:
  0.0 255.7 jit_solution(16825119779834685522)
XLA Ops:
  0.7 3.1 %slice_bitcast_fusion.8 = (f32[2,256,256]{2,1,0:T(8,128)}, f32[2,256,256]{2,1,0:T(8,128)}, f32[2,256,256]{2,1,0:T(8,128)}, f32[2,256,256]{2,1,0:T(8,128)}) fusion(f32[2,2,512,256]{3,2,1,0:T(8,128)} %own.5), kind=kLoop, calls=%fused_computation.21 | loop fusion | bytes 4194304 | tf_op jit(solution)/shard_map/squeeze | solution.py:262
  3.7 4.5 %collective-permute-start = (f32[2,256,256]{2,1,0:T(8,128)}, f32[2,256,256]{2,1,0:T(8,128)S(1)}, u32[]{:S(2)}, u32[]{:S(2)}) collective-permute-start(f32[2,256,256]{2,1,0:T(8,128)} %get-tuple-element.23), channel_id=1, source_target_pairs={{1,0},{2,1},{3,2},{4,3},{5,4},{6,5},{7,6},{8,7},{9,8},{10,9},{11,1... | collective-permute-start | bytes 1572872 | tf_op jit(solution)/shard_map/ppermute | solution.py:220
  8.2 1.3 collective-permute-start.2
  9.5 2.7 %collective-permute-start.4 = (f32[2,256,256]{2,1,0:T(8,128)}, f32[2,256,256]{2,1,0:T(8,128)}, u32[]{:S(2)}, u32[]{:S(2)}) collective-permute-start(f32[2,256,256]{2,1,0:T(8,128)} %get-tuple-element.22), channel_id=1, source_target_pairs={{1,0},{2,1},{3,2},{4,3},{5,4},{6,5},{7,6},{8,7},{9,8},{10,9},{11,1... | collective-permute-start | bytes 1572872 | tf_op jit(solution)/shard_map/ppermute | solution.py:220
  12.2 2.4 collective-permute-start.1
  14.5 11.9 %collective-permute-done.right_top = f32[2,256,256]{2,1,0:T(8,128)S(1)} collective-permute-done((f32[2,256,256]{2,1,0:T(8,128)}, f32[2,256,256]{2,1,0:T(8,128)S(1)}, u32[]{:S(2)}, u32[]{:S(2)}) %collective-permute-start) | collective-permute-done | bytes 524320 | tf_op jit(solution)/shard_map/ppermute | solution.py:220
  26.4 1.3 collective-permute-start.3
  27.7 1.3 collective-permute-start.6
  29.8 1.0 cosine_bitcast_fusion
  30.8 6.5 %collective-permute-start.5 = (f32[2,256,256]{2,1,0:T(8,128)}, f32[2,256,256]{2,1,0:T(8,128)S(1)}, u32[]{:S(2)}, u32[]{:S(2)}) collective-permute-start(f32[2,256,256]{2,1,0:T(8,128)} %get-tuple-element.21), channel_id=1, source_target_pairs={{1,0},{2,1},{3,2},{4,3},{5,4},{6,5},{7,6},{8,7},{9,8},{10,9},{11,1... | collective-permute-start | bytes 1572872 | tf_op jit(solution)/shard_map/ppermute | solution.py:220
  37.4 17.1 %collective-permute-done.4.right_top = f32[2,256,256]{2,1,0:T(8,128)} collective-permute-done((f32[2,256,256]{2,1,0:T(8,128)}, f32[2,256,256]{2,1,0:T(8,128)}, u32[]{:S(2)}, u32[]{:S(2)}) %collective-permute-start.4) | collective-permute-done | bytes 524320 | tf_op jit(solution)/shard_map/ppermute | solution.py:220
  54.5 1.3 collective-permute-start.7
  55.8 9.9 %collective-permute-done.1.right_bottom = f32[2,256,256]{2,1,0:T(8,128)} collective-permute-done((f32[2,256,256]{2,1,0:T(8,128)}, f32[2,256,256]{2,1,0:T(8,128)}, u32[]{:S(2)}, u32[]{:S(2)}) %collective-permute-start.1) | collective-permute-done | bytes 524320 | tf_op jit(solution)/shard_map/ppermute | solution.py:220
  65.8 1.6 copy-done.8
  67.4 7.9 %arrive.1.arriving = f32[4,2,256,256]{3,2,1,0:T(8,128)S(1)} custom-call(s32[1,1]{1,0:T(1,128)S(6)} %copy.12.count, s32[4,2]{1,0:T(4,128)S(1)} %copy.11.offsets, f32[2,2,512,256]{3,2,1,0:T(8,128)S(1)} %copy-done, f32[2,256,256]{2,1,0:T(8,128)S(1)} %collective-permute-done.right_top, f32[2,256,256]{2,1,0:T(8,128)} %collective-permute-done.1.right_bottom, ...), custom_call_target="tpu_custom_call" | custom-call | flops 6442450944 | bytes 8388608 | tf_op jit(solution)/shard_map/arrive/pallas_call | solution.py:194
  75.3 0.5 collective-permute-done.5.right_bottom
  75.9 9.7 %misfit.1 = (f32[2,3,2,256,256]{4,3,2,1,0:T(8,128)}, f32[4,2,256,256]{3,2,1,0:T(8,128)S(1)}) custom-call(s32[1,1]{1,0:T(1,128)S(6)} %copy.12.count, s32[4,2]{1,0:T(4,128)S(1)} %copy.11.offsets, f32[2,2,512,256]{3,2,1,0:T(8,128)S(1)} %copy-done, f32[2,256,256]{2,1,0:T(8,128)} %collective-permute-done.4.right_top, ...), custom_call_target="tpu_custom_call" | custom-call | flops 6442450944 | bytes 8388608 | tf_op jit(solution)/shard_map/misfit/pallas_call | solution.py:194
  85.6 8.6 %leave.1 = (f32[2,3,2,256,256]{4,3,2,1,0:T(8,128)S(1)}, f32[2,256,256]{2,1,0:T(8,128)S(1)}) custom-call(s32[1,1]{1,0:T(1,128)S(6)} %copy.12.count, s32[4,2]{1,0:T(4,128)S(1)} %copy.11.offsets, f32[2,2,512,256]{3,2,1,0:T(8,128)S(1)} %copy-done.1, f32[2,256,256]{2,1,0:T(8,128)S(1)} %copy-done.7, f32[2,256,256]{2,1,0:T(8,128)} %collective-permute-done.1.right_bottom, ...), custom_call_target="tpu_custom_call" | custom-call | flops 6442450944 | bytes 8388608 | tf_op jit(solution)/shard_map/leave/pallas_call | solution.py:194
  94.2 0.8 copy-done.2
  95.0 19.4 %collective-permute-start.16 = (f32[256,256]{1,0:T(8,128)S(1)}, f32[256,256]{1,0:T(8,128)}, u32[]{:S(2)}, u32[]{:S(2)}) collective-permute-start(f32[256,256]{1,0:T(8,128)S(1)} %select_bitcast_fusion), channel_id=1, source_target_pairs={{0,32},{32,0},{64,96},{96,64},{128,160},{160,128},{192,224},{224,1... | collective-permute-start | bytes 786440 | tf_op jit(solution)/shard_map/ppermute | solution.py:224
  114.4 1.3 collective-permute-done.16
  115.7 1.2 bitcast_add_fusion.6
  116.9 0.7 slice_select_fusion
  117.5 6.0 %collective-permute-done.17 = f32[128,256]{1,0:T(8,128)S(1)} collective-permute-done((f32[128,256]{1,0:T(8,128)}, f32[128,256]{1,0:T(8,128)S(1)}, u32[]{:S(2)}, u32[]{:S(2)}) %collective-permute-start.17) | collective-permute-done | bytes 131104 | tf_op jit(solution)/shard_map/ppermute | solution.py:224
  123.6 20.4 %collective-permute-start.18 = (f32[64,256]{1,0:T(8,128)S(1)}, f32[64,256]{1,0:T(8,128)S(1)}, u32[]{:S(2)}, u32[]{:S(2)}) collective-permute-start(f32[64,256]{1,0:T(8,128)S(1)} %slice_select_fusion.1), channel_id=1, source_target_pairs={{0,8},{1,9},{2,10},{3,11},{4,12},{5,13},{6,14},{7,15},{8,0},{9,1},... | collective-permute-start | bytes 196616 | tf_op jit(solution)/shard_map/ppermute | solution.py:224
  144.0 2.2 collective-permute-done.18
  146.4 1.5 slice_bitcast_fusion.2
  147.8 1.6 collective-permute-start.13
  149.4 2.7 %collective-permute-done.19 = f32[64,256]{1,0:T(8,128)S(1)} collective-permute-done((f32[64,256]{1,0:T(8,128)S(1)}, f32[64,256]{1,0:T(8,128)S(1)}, u32[]{:S(2)}, u32[]{:S(2)}) %collective-permute-start.19) | collective-permute-done | bytes 65568 | tf_op jit(solution)/shard_map/ppermute | solution.py:224
  152.2 5.8 %collective-permute-done.20 = f32[64,256]{1,0:T(8,128)S(1)} collective-permute-done((f32[64,256]{1,0:T(8,128)S(1)}, f32[64,256]{1,0:T(8,128)S(1)}, u32[]{:S(2)}, u32[]{:S(2)}) %collective-permute-start.20) | collective-permute-done | bytes 65568 | tf_op jit(solution)/shard_map/ppermute | solution.py:224
  158.3 4.3 %collective-permute-done.21 = f32[64,256]{1,0:T(8,128)S(1)} collective-permute-done((f32[64,256]{1,0:T(8,128)S(1)}, f32[64,256]{1,0:T(8,128)S(1)}, u32[]{:S(2)}, u32[]{:S(2)}) %collective-permute-start.21) | collective-permute-done | bytes 65568 | tf_op jit(solution)/shard_map/ppermute | solution.py:224
  162.6 4.1 %collective-permute-start.12 = (f32[2,256,256]{2,1,0:T(8,128)S(1)}, f32[2,256,256]{2,1,0:T(8,128)S(1)}, u32[]{:S(2)}, u32[]{:S(2)}) collective-permute-start(f32[2,256,256]{2,1,0:T(8,128)S(1)} %get-tuple-element.17), channel_id=1, source_target_pairs={{0,32},{32,64},{64,96},{96,128},{128,160},{160,192},{192,224},{1,3... | collective-permute-start | bytes 1572872 | tf_op jit(solution)/shard_map/ppermute | solution.py:220
  166.7 2.4 collective-permute-start.15
  169.2 8.2 %collective-permute-start.23 = (f32[64,256]{1,0:T(8,128)S(1)}, f32[64,256]{1,0:T(8,128)S(1)}, u32[]{:S(2)}, u32[]{:S(2)}) collective-permute-start(f32[64,256]{1,0:T(8,128)S(1)} %add.62), channel_id=1, source_target_pairs={{0,128},{32,160},{64,192},{96,224},{128,0},{160,32},{192,64},{224,... | collective-permute-start | bytes 196616 | tf_op jit(solution)/shard_map/ppermute | solution.py:224
  177.5 3.4 %collective-permute-start.9 = (f32[2,256,256]{2,1,0:T(8,128)S(1)}, f32[2,256,256]{2,1,0:T(8,128)S(1)}, u32[]{:S(2)}, u32[]{:S(2)}) collective-permute-start(f32[2,256,256]{2,1,0:T(8,128)S(1)} %get-tuple-element.14), channel_id=1, source_target_pairs={{0,32},{32,64},{64,96},{96,128},{128,160},{160,192},{192,224},{1,3... | collective-permute-start | bytes 1572872 | tf_op jit(solution)/shard_map/ppermute | solution.py:220
  180.9 1.9 collective-permute-start.11
  182.8 0.5 collective-permute-start.24
  183.4 3.8 %collective-permute-done.24 = f32[64,256]{1,0:T(8,128)S(1)} collective-permute-done((f32[64,256]{1,0:T(8,128)S(1)}, f32[64,256]{1,0:T(8,128)S(1)}, u32[]{:S(2)}, u32[]{:S(2)}) %collective-permute-start.24) | collective-permute-done | bytes 65568 | tf_op jit(solution)/shard_map/ppermute | solution.py:224
  187.2 3.1 %collective-permute-start.14 = (f32[2,256,256]{2,1,0:T(8,128)S(1)}, f32[2,256,256]{2,1,0:T(8,128)S(1)}, u32[]{:S(2)}, u32[]{:S(2)}) collective-permute-start(f32[2,256,256]{2,1,0:T(8,128)S(1)} %bitcast_add_fusion.1), channel_id=1, source_target_pairs={{0,1},{1,2},{2,3},{3,4},{4,5},{5,6},{6,7},{7,8},{8,9},{9,10},{10,1... | collective-permute-start | bytes 1572872 | tf_op jit(solution)/shard_map/ppermute | solution.py:220
  190.3 10.5 %collective-permute-start.25 = (f32[128,256]{1,0:T(8,128)S(1)}, f32[128,256]{1,0:T(8,128)S(1)}, u32[]{:S(2)}, u32[]{:S(2)}) collective-permute-start(f32[128,256]{1,0:T(8,128)S(1)} %pad_maximum_fusion.4), channel_id=1, source_target_pairs={{0,1},{1,0},{2,3},{3,2},{4,5},{5,4},{6,7},{7,6},{8,9},{9,8},{10,11... | collective-permute-start | bytes 393224 | tf_op jit(solution)/shard_map/ppermute | solution.py:224
  200.9 2.2 collective-permute-start.8
  203.1 2.9 %collective-permute-done.25 = f32[128,256]{1,0:T(8,128)S(1)} collective-permute-done((f32[128,256]{1,0:T(8,128)S(1)}, f32[128,256]{1,0:T(8,128)S(1)}, u32[]{:S(2)}, u32[]{:S(2)}) %collective-permute-start.25) | collective-permute-done | bytes 131104 | tf_op jit(solution)/shard_map/ppermute | solution.py:224
  206.0 4.4 %collective-permute-start.10 = (f32[2,256,256]{2,1,0:T(8,128)S(1)}, f32[2,256,256]{2,1,0:T(8,128)S(1)}, u32[]{:S(2)}, u32[]{:S(2)}) collective-permute-start(f32[2,256,256]{2,1,0:T(8,128)S(1)} %bitcast_add_fusion.4), channel_id=1, source_target_pairs={{0,1},{1,2},{2,3},{3,4},{4,5},{5,6},{6,7},{7,8},{8,9},{9,10},{10,1... | collective-permute-start | bytes 1572872 | tf_op jit(solution)/shard_map/ppermute | solution.py:220
  210.5 2.8 %collective-permute-start.26 = (f32[256,256]{1,0:T(8,128)S(1)}, f32[256,256]{1,0:T(8,128)S(1)}, u32[]{:S(2)}, u32[]{:S(2)}) collective-permute-start(f32[256,256]{1,0:T(8,128)S(1)} %pad_maximum_fusion.3), channel_id=1, source_target_pairs={{0,32},{32,0},{64,96},{96,64},{128,160},{160,128},{192,224},{224,1... | collective-permute-start | bytes 786440 | tf_op jit(solution)/shard_map/ppermute | solution.py:224
  213.2 22.7 %collective-permute-done.14 = f32[2,256,256]{2,1,0:T(8,128)S(1)} collective-permute-done((f32[2,256,256]{2,1,0:T(8,128)S(1)}, f32[2,256,256]{2,1,0:T(8,128)S(1)}, u32[]{:S(2)}, u32[]{:S(2)}) %collective-permute-start.14) | collective-permute-done | bytes 524320 | tf_op jit(solution)/shard_map/ppermute | solution.py:220
  236.1 16.9 %collective-permute-done.10 = f32[2,256,256]{2,1,0:T(8,128)S(1)} collective-permute-done((f32[2,256,256]{2,1,0:T(8,128)S(1)}, f32[2,256,256]{2,1,0:T(8,128)S(1)}, u32[]{:S(2)}, u32[]{:S(2)}) %collective-permute-start.10) | collective-permute-done | bytes 524320 | tf_op jit(solution)/shard_map/ppermute | solution.py:220
  253.4 1.5 pad_maximum_fusion
  254.9 0.8 pad_maximum_fusion.2
  (64 shorter events, 1.7 us)
Async XLA Ops:
  0.6 65.1 %copy-start = (f32[2,2,512,256]{3,2,1,0:T(8,128)S(1)}, f32[2,2,512,256]{3,2,1,0:T(8,128)}, u32[]{:S(2)}) copy-start(f32[2,2,512,256]{3,2,1,0:T(8,128)} %own.5) | copy-start | bytes 6291460
  0.6 28.4 %copy-start.12 = (s32[1,1,4,2]{2,3,1,0:T(2,128)S(1)}, s32[1,1,4,2]{2,3,1,0:T(2,128)}, u32[]{:S(2)}) copy-start(s32[1,1,4,2]{2,3,1,0:T(2,128)} %param.11) | copy-start | bytes 100
  0.7 29.1 %copy-start.11 = (f32[256,256]{1,0:T(8,128)S(1)}, f32[256,256]{1,0:T(8,128)}, u32[]{:S(2)}) copy-start(f32[256,256]{1,0:T(8,128)} %param.9) | copy-start | bytes 786436
  0.7 65.1 %copy-start.4 = (f32[2,256,256]{2,1,0:T(8,128)S(1)}, f32[2,256,256]{2,1,0:T(8,128)}, u32[]{:S(2)}) copy-start(f32[2,256,256]{2,1,0:T(8,128)} %probe.3) | copy-start | bytes 1572868
  3.7 22.7 %collective-permute-start = (f32[2,256,256]{2,1,0:T(8,128)}, f32[2,256,256]{2,1,0:T(8,128)S(1)}, u32[]{:S(2)}, u32[]{:S(2)}) collective-permute-start(f32[2,256,256]{2,1,0:T(8,128)} %get-tuple-element.23), channel_id=1, source_target_pairs={{1,0},{2,1},{3,2},{4,3},{5,4},{6,5},{7,6},{8,7},{9,8},{10,9},{11,1... | collective-permute-start | bytes 1572872 | tf_op jit(solution)/shard_map/ppermute | solution.py:220
  8.2 22.6 %collective-permute-start.2 = (f32[2,256,256]{2,1,0:T(8,128)}, f32[2,256,256]{2,1,0:T(8,128)}, u32[]{:S(2)}, u32[]{:S(2)}) collective-permute-start(f32[2,256,256]{2,1,0:T(8,128)} %get-tuple-element.23), channel_id=1, source_target_pairs={{32,0},{64,32},{96,64},{128,96},{160,128},{192,160},{224,192},{33,... | collective-permute-start | bytes 1572872 | tf_op jit(solution)/shard_map/ppermute | solution.py:220
  9.5 45.0 %collective-permute-start.4 = (f32[2,256,256]{2,1,0:T(8,128)}, f32[2,256,256]{2,1,0:T(8,128)}, u32[]{:S(2)}, u32[]{:S(2)}) collective-permute-start(f32[2,256,256]{2,1,0:T(8,128)} %get-tuple-element.22), channel_id=1, source_target_pairs={{1,0},{2,1},{3,2},{4,3},{5,4},{6,5},{7,6},{8,7},{9,8},{10,9},{11,1... | collective-permute-start | bytes 1572872 | tf_op jit(solution)/shard_map/ppermute | solution.py:220
  12.2 53.6 %collective-permute-start.1 = (f32[2,256,256]{2,1,0:T(8,128)}, f32[2,256,256]{2,1,0:T(8,128)}, u32[]{:S(2)}, u32[]{:S(2)}) collective-permute-start(f32[2,256,256]{2,1,0:T(8,128)} %get-tuple-element.20), channel_id=1, source_target_pairs={{1,0},{2,1},{3,2},{4,3},{5,4},{6,5},{7,6},{8,7},{9,8},{10,9},{11,1... | collective-permute-start | bytes 1572872 | tf_op jit(solution)/shard_map/ppermute | solution.py:220
  26.4 48.9 %copy-start.6 = (f32[2,256,256]{2,1,0:T(8,128)}, f32[2,256,256]{2,1,0:T(8,128)S(1)}, u32[]{:S(2)}) copy-start(f32[2,256,256]{2,1,0:T(8,128)S(1)} %collective-permute-done.right_top) | copy-start | bytes 1572868
  26.4 39.3 %collective-permute-start.3 = (f32[2,256,256]{2,1,0:T(8,128)S(1)}, f32[2,256,256]{2,1,0:T(8,128)}, u32[]{:S(2)}, u32[]{:S(2)}) collective-permute-start(f32[2,256,256]{2,1,0:T(8,128)S(1)} %collective-permute-done.right_top), channel_id=1, source_target_pairs={{32,0},{64,32},{96,64},{128,96},{160,128},{192,160},{224,192},{33,... | collective-permute-start | bytes 1572872 | tf_op jit(solution)/shard_map/ppermute | solution.py:220
  27.7 47.6 %collective-permute-start.6 = (f32[2,256,256]{2,1,0:T(8,128)}, f32[2,256,256]{2,1,0:T(8,128)}, u32[]{:S(2)}, u32[]{:S(2)}) collective-permute-start(f32[2,256,256]{2,1,0:T(8,128)} %get-tuple-element.22), channel_id=1, source_target_pairs={{32,0},{64,32},{96,64},{128,96},{160,128},{192,160},{224,192},{33,... | collective-permute-start | bytes 1572872 | tf_op jit(solution)/shard_map/ppermute | solution.py:220
  30.8 45.0 %copy-start.3 = (f32[1,1,4,256,256]{4,3,2,1,0:T(8,128)S(1)}, f32[1,1,4,256,256]{4,3,2,1,0:T(8,128)}, u32[]{:S(2)}) copy-start(f32[1,1,4,256,256]{4,3,2,1,0:T(8,128)} %param.12) | copy-start | bytes 3145732
  30.8 45.0 %collective-permute-start.5 = (f32[2,256,256]{2,1,0:T(8,128)}, f32[2,256,256]{2,1,0:T(8,128)S(1)}, u32[]{:S(2)}, u32[]{:S(2)}) collective-permute-start(f32[2,256,256]{2,1,0:T(8,128)} %get-tuple-element.21), channel_id=1, source_target_pairs={{1,0},{2,1},{3,2},{4,3},{5,4},{6,5},{7,6},{8,7},{9,8},{10,9},{11,1... | collective-permute-start | bytes 1572872 | tf_op jit(solution)/shard_map/ppermute | solution.py:220
  54.5 21.3 %collective-permute-start.7 = (f32[2,256,256]{2,1,0:T(8,128)}, f32[2,256,256]{2,1,0:T(8,128)S(1)}, u32[]{:S(2)}, u32[]{:S(2)}) collective-permute-start(f32[2,256,256]{2,1,0:T(8,128)} %collective-permute-done.4.right_top), channel_id=1, source_target_pairs={{32,0},{64,32},{96,64},{128,96},{160,128},{192,160},{224,192},{33,... | collective-permute-start | bytes 1572872 | tf_op jit(solution)/shard_map/ppermute | solution.py:220
  65.8 1.6 copy-start.8
  67.4 8.5 %copy-start.9 = (bf16[2,2,512,512]{3,2,1,0:T(8,128)(2,1)S(1)}, bf16[2,2,512,512]{3,2,1,0:T(8,128)(2,1)}, u32[]{:S(2)}) copy-start(bf16[2,2,512,512]{3,2,1,0:T(8,128)(2,1)} %constant.17.clone.tables) | copy-start | bytes 6291460
  75.9 9.7 %copy-start.1 = (f32[2,2,512,256]{3,2,1,0:T(8,128)S(1)}, f32[2,2,512,256]{3,2,1,0:T(8,128)}, u32[]{:S(2)}) copy-start(f32[2,2,512,256]{3,2,1,0:T(8,128)} %own.5) | copy-start | bytes 6291460
  75.9 9.7 %copy-start.5 = (f32[2,256,256]{2,1,0:T(8,128)S(1)}, f32[2,256,256]{2,1,0:T(8,128)}, u32[]{:S(2)}) copy-start(f32[2,256,256]{2,1,0:T(8,128)} %probe.3) | copy-start | bytes 1572868
  75.9 9.7 %copy-start.7 = (f32[2,256,256]{2,1,0:T(8,128)S(1)}, f32[2,256,256]{2,1,0:T(8,128)}, u32[]{:S(2)}) copy-start(f32[2,256,256]{2,1,0:T(8,128)} %copy-done.6) | copy-start | bytes 1572868
  94.2 0.8 copy-start.2
  95.0 20.7 %collective-permute-start.16 = (f32[256,256]{1,0:T(8,128)S(1)}, f32[256,256]{1,0:T(8,128)}, u32[]{:S(2)}, u32[]{:S(2)}) collective-permute-start(f32[256,256]{1,0:T(8,128)S(1)} %select_bitcast_fusion), channel_id=1, source_target_pairs={{0,32},{32,0},{64,96},{96,64},{128,160},{160,128},{192,224},{224,1... | collective-permute-start | bytes 786440 | tf_op jit(solution)/shard_map/ppermute | solution.py:224
  117.5 6.0 %collective-permute-start.17 = (f32[128,256]{1,0:T(8,128)}, f32[128,256]{1,0:T(8,128)S(1)}, u32[]{:S(2)}, u32[]{:S(2)}) collective-permute-start(f32[128,256]{1,0:T(8,128)} %slice_select_fusion), channel_id=1, source_target_pairs={{0,1},{1,0},{2,3},{3,2},{4,5},{5,4},{6,7},{7,6},{8,9},{9,8},{10,11... | collective-permute-start | bytes 393224 | tf_op jit(solution)/shard_map/ppermute | solution.py:224
  123.6 22.7 %collective-permute-start.18 = (f32[64,256]{1,0:T(8,128)S(1)}, f32[64,256]{1,0:T(8,128)S(1)}, u32[]{:S(2)}, u32[]{:S(2)}) collective-permute-start(f32[64,256]{1,0:T(8,128)S(1)} %slice_select_fusion.1), channel_id=1, source_target_pairs={{0,8},{1,9},{2,10},{3,11},{4,12},{5,13},{6,14},{7,15},{8,0},{9,1},... | collective-permute-start | bytes 196616 | tf_op jit(solution)/shard_map/ppermute | solution.py:224
  146.3 5.9 %collective-permute-start.19 = (f32[64,256]{1,0:T(8,128)S(1)}, f32[64,256]{1,0:T(8,128)S(1)}, u32[]{:S(2)}, u32[]{:S(2)}) collective-permute-start(f32[64,256]{1,0:T(8,128)S(1)} %select_add_fusion.1), channel_id=1, source_target_pairs={{0,2},{1,3},{2,0},{3,1},{4,6},{5,7},{6,4},{7,5},{8,10},{9,11},{10,... | collective-permute-start | bytes 196616 | tf_op jit(solution)/shard_map/ppermute | solution.py:224
  147.8 35.5 %copy-start.10 = (f32[2,3,2,256,256]{4,3,2,1,0:T(8,128)S(1)}, f32[2,3,2,256,256]{4,3,2,1,0:T(8,128)}, u32[]{:S(2)}) copy-start(f32[2,3,2,256,256]{4,3,2,1,0:T(8,128)} %get-tuple-element.8) | copy-start | bytes 9437188
  147.8 35.0 %collective-permute-start.13 = (f32[2,256,256]{2,1,0:T(8,128)S(1)}, f32[2,256,256]{2,1,0:T(8,128)S(1)}, u32[]{:S(2)}, u32[]{:S(2)}) collective-permute-start(f32[2,256,256]{2,1,0:T(8,128)S(1)} %get-tuple-element.19), channel_id=1, source_target_pairs={{0,32},{32,64},{64,96},{96,128},{128,160},{160,192},{192,224},{1,3... | collective-permute-start | bytes 1572872 | tf_op jit(solution)/shard_map/ppermute | solution.py:220
  152.1 5.9 %collective-permute-start.20 = (f32[64,256]{1,0:T(8,128)S(1)}, f32[64,256]{1,0:T(8,128)S(1)}, u32[]{:S(2)}, u32[]{:S(2)}) collective-permute-start(f32[64,256]{1,0:T(8,128)S(1)} %add.59), channel_id=1, source_target_pairs={{0,16},{1,17},{2,18},{3,19},{4,20},{5,21},{6,22},{7,23},{8,24},{9,... | collective-permute-start | bytes 196616 | tf_op jit(solution)/shard_map/ppermute | solution.py:224
  158.0 4.5 %collective-permute-start.21 = (f32[64,256]{1,0:T(8,128)S(1)}, f32[64,256]{1,0:T(8,128)S(1)}, u32[]{:S(2)}, u32[]{:S(2)}) collective-permute-start(f32[64,256]{1,0:T(8,128)S(1)} %add.60), channel_id=1, source_target_pairs={{0,4},{1,5},{2,6},{3,7},{4,0},{5,1},{6,2},{7,3},{8,12},{9,13},{10,... | collective-permute-start | bytes 196616 | tf_op jit(solution)/shard_map/ppermute | solution.py:224
  162.5 6.6 %collective-permute-start.22 = (f32[64,256]{1,0:T(8,128)S(1)}, f32[64,256]{1,0:T(8,128)S(1)}, u32[]{:S(2)}, u32[]{:S(2)}) collective-permute-start(f32[64,256]{1,0:T(8,128)S(1)} %add.61), channel_id=1, source_target_pairs={{0,64},{32,96},{64,0},{96,32},{128,192},{160,224},{192,128},{224,1... | collective-permute-start | bytes 196616 | tf_op jit(solution)/shard_map/ppermute | solution.py:224
  162.6 38.3 %collective-permute-start.12 = (f32[2,256,256]{2,1,0:T(8,128)S(1)}, f32[2,256,256]{2,1,0:T(8,128)S(1)}, u32[]{:S(2)}, u32[]{:S(2)}) collective-permute-start(f32[2,256,256]{2,1,0:T(8,128)S(1)} %get-tuple-element.17), channel_id=1, source_target_pairs={{0,32},{32,64},{64,96},{96,128},{128,160},{160,192},{192,224},{1,3... | collective-permute-start | bytes 1572872 | tf_op jit(solution)/shard_map/ppermute | solution.py:220
  166.7 43.7 %collective-permute-start.15 = (f32[2,256,256]{2,1,0:T(8,128)S(1)}, f32[2,256,256]{2,1,0:T(8,128)S(1)}, u32[]{:S(2)}, u32[]{:S(2)}) collective-permute-start(f32[2,256,256]{2,1,0:T(8,128)S(1)} %get-tuple-element.18), channel_id=1, source_target_pairs={{0,1},{1,2},{2,3},{3,4},{4,5},{5,6},{6,7},{7,8},{8,9},{9,10},{10,1... | collective-permute-start | bytes 1572872 | tf_op jit(solution)/shard_map/ppermute | solution.py:220
  169.2 11.7 %collective-permute-start.23 = (f32[64,256]{1,0:T(8,128)S(1)}, f32[64,256]{1,0:T(8,128)S(1)}, u32[]{:S(2)}, u32[]{:S(2)}) collective-permute-start(f32[64,256]{1,0:T(8,128)S(1)} %add.62), channel_id=1, source_target_pairs={{0,128},{32,160},{64,192},{96,224},{128,0},{160,32},{192,64},{224,... | collective-permute-start | bytes 196616 | tf_op jit(solution)/shard_map/ppermute | solution.py:224
  177.5 12.9 %collective-permute-start.9 = (f32[2,256,256]{2,1,0:T(8,128)S(1)}, f32[2,256,256]{2,1,0:T(8,128)S(1)}, u32[]{:S(2)}, u32[]{:S(2)}) collective-permute-start(f32[2,256,256]{2,1,0:T(8,128)S(1)} %get-tuple-element.14), channel_id=1, source_target_pairs={{0,32},{32,64},{64,96},{96,128},{128,160},{160,192},{192,224},{1,3... | collective-permute-start | bytes 1572872 | tf_op jit(solution)/shard_map/ppermute | solution.py:220
  180.9 55.3 %collective-permute-start.11 = (f32[2,256,256]{2,1,0:T(8,128)S(1)}, f32[2,256,256]{2,1,0:T(8,128)S(1)}, u32[]{:S(2)}, u32[]{:S(2)}) collective-permute-start(f32[2,256,256]{2,1,0:T(8,128)S(1)} %get-tuple-element.13), channel_id=1, source_target_pairs={{0,1},{1,2},{2,3},{3,4},{4,5},{5,6},{6,7},{7,8},{8,9},{9,10},{10,1... | collective-permute-start | bytes 1572872 | tf_op jit(solution)/shard_map/ppermute | solution.py:220
  182.8 4.4 %collective-permute-start.24 = (f32[64,256]{1,0:T(8,128)S(1)}, f32[64,256]{1,0:T(8,128)S(1)}, u32[]{:S(2)}, u32[]{:S(2)}) collective-permute-start(f32[64,256]{1,0:T(8,128)S(1)} %add.63), channel_id=1, source_target_pairs={{0,8},{1,9},{2,10},{3,11},{4,12},{5,13},{6,14},{7,15},{8,0},{9,1},... | collective-permute-start | bytes 196616 | tf_op jit(solution)/shard_map/ppermute | solution.py:224
  187.2 48.7 %collective-permute-start.14 = (f32[2,256,256]{2,1,0:T(8,128)S(1)}, f32[2,256,256]{2,1,0:T(8,128)S(1)}, u32[]{:S(2)}, u32[]{:S(2)}) collective-permute-start(f32[2,256,256]{2,1,0:T(8,128)S(1)} %bitcast_add_fusion.1), channel_id=1, source_target_pairs={{0,1},{1,2},{2,3},{3,4},{4,5},{5,6},{6,7},{7,8},{8,9},{9,10},{10,1... | collective-permute-start | bytes 1572872 | tf_op jit(solution)/shard_map/ppermute | solution.py:220
  190.3 15.7 %collective-permute-start.25 = (f32[128,256]{1,0:T(8,128)S(1)}, f32[128,256]{1,0:T(8,128)S(1)}, u32[]{:S(2)}, u32[]{:S(2)}) collective-permute-start(f32[128,256]{1,0:T(8,128)S(1)} %pad_maximum_fusion.4), channel_id=1, source_target_pairs={{0,1},{1,0},{2,3},{3,2},{4,5},{5,4},{6,7},{7,6},{8,9},{9,8},{10,11... | collective-permute-start | bytes 393224 | tf_op jit(solution)/shard_map/ppermute | solution.py:224
  200.9 35.2 %collective-permute-start.8 = (f32[2,256,256]{2,1,0:T(8,128)S(1)}, f32[2,256,256]{2,1,0:T(8,128)S(1)}, u32[]{:S(2)}, u32[]{:S(2)}) collective-permute-start(f32[2,256,256]{2,1,0:T(8,128)S(1)} %get-tuple-element.12), channel_id=1, source_target_pairs={{0,32},{32,64},{64,96},{96,128},{128,160},{160,192},{192,224},{1,3... | collective-permute-start | bytes 1572872 | tf_op jit(solution)/shard_map/ppermute | solution.py:220
  206.0 47.0 %collective-permute-start.10 = (f32[2,256,256]{2,1,0:T(8,128)S(1)}, f32[2,256,256]{2,1,0:T(8,128)S(1)}, u32[]{:S(2)}, u32[]{:S(2)}) collective-permute-start(f32[2,256,256]{2,1,0:T(8,128)S(1)} %bitcast_add_fusion.4), channel_id=1, source_target_pairs={{0,1},{1,2},{2,3},{3,4},{4,5},{5,6},{6,7},{7,8},{8,9},{9,10},{10,1... | collective-permute-start | bytes 1572872 | tf_op jit(solution)/shard_map/ppermute | solution.py:220
  210.5 44.4 %collective-permute-start.26 = (f32[256,256]{1,0:T(8,128)S(1)}, f32[256,256]{1,0:T(8,128)S(1)}, u32[]{:S(2)}, u32[]{:S(2)}) collective-permute-start(f32[256,256]{1,0:T(8,128)S(1)} %pad_maximum_fusion.3), channel_id=1, source_target_pairs={{0,32},{32,0},{64,96},{96,64},{128,160},{160,128},{192,224},{224,1... | collective-permute-start | bytes 786440 | tf_op jit(solution)/shard_map/ppermute | solution.py:224

commit v2 on v1

--- a/solution.py
+++ b/solution.py
@@ -15,17 +15,20 @@
 
 
 def dft_blocks(window):
-    indices = np.arange(window)
-    angles = 2.0 * math.pi / window * (indices[:, None] * indices[None, :] % window)
-    cos, sin = np.cos(angles) / math.sqrt(window), np.sin(angles) / math.sqrt(window)
-    ahead = np.block([[cos, -sin], [sin, cos]])
-    behind = np.block([[cos, sin], [-sin, cos]])
-    parts = []
-    for table in (ahead, behind):
-        high = table.astype(ml_dtypes.bfloat16)
-        low = (table - high.astype(np.float64)).astype(ml_dtypes.bfloat16)
-        parts.append(np.stack([high, low]))
-    return np.stack(parts)
+    half = window // 2
+    places, turns = np.arange(half)[:, None], np.arange(half)[None, :]
+    forms = []
+    for parity in range(2):
+        angles = 2.0 * math.pi / window * (places * (2 * turns + parity) % window)
+        cos, sin = np.cos(angles) / math.sqrt(window), np.sin(angles) / math.sqrt(window)
+        forms.append(np.block([[cos, -sin], [sin, cos]]))
+    tables = []
+    for form in (forms, [np.transpose(form) for form in forms]):
+        form = np.stack(form)
+        high = form.astype(ml_dtypes.bfloat16)
+        low = (form - high.astype(np.float64)).astype(ml_dtypes.bfloat16)
+        tables.append(np.stack([high, low], axis=1))
+    return np.stack(tables)
 
 
 def halves(value):
@@ -37,26 +40,78 @@
     return jnp.dot(left, right, preferred_element_type=jnp.float32)
 
 
-def along_columns(wave, table):
-    window = wave[0].shape[0]
-    high, low = halves(jnp.concatenate(wave, axis=1))
-    out = dot(high, table[0]) + dot(low, table[0]) + dot(high, table[1])
-    return out[:, :window], out[:, window:]
-
-
-def along_rows(wave, table):
-    window = wave[0].shape[0]
-    high, low = halves(jnp.concatenate(wave, axis=0))
-    out = dot(table[0], high) + dot(table[0], low) + dot(table[1], high)
-    return out[:window], out[window:]
+def apply(value, table, axis):
+    high, low = halves(value)
+    if axis:
+        return dot(high, table[0]) + dot(low, table[0]) + dot(high, table[1])
+    return dot(table[0], high) + dot(table[0], low) + dot(table[1], high)
+
+
+def cleave(value, axis):
+    half = value.shape[axis] // 2
+    if axis:
+        return value[:, :half], value[:, half:]
+    return value[:half], value[half:]
+
+
+def apart(wave, tables, axis):
+    pairs = [cleave(part, axis) for part in wave]
+    even = jnp.concatenate([first + second for first, second in pairs], axis=axis)
+    odd = jnp.concatenate([first - second for first, second in pairs], axis=axis)
+    even = cleave(apply(even, tables.at[0], axis), axis)
+    odd = cleave(apply(odd, tables.at[1], axis), axis)
+    return tuple(jnp.concatenate(pair, axis=axis) for pair in zip(even, odd))
+
+
+def together(wave, tables, axis):
+    even, odd = zip(*(cleave(part, axis) for part in wave))
+    even = cleave(apply(jnp.concatenate(even, axis=axis), tables.at[0], axis), axis)
+    odd = cleave(apply(jnp.concatenate(odd, axis=axis), tables.at[1], axis), axis)
+    return tuple(
+        jnp.concatenate([first + second, first - second], axis=axis)
+        for first, second in zip(even, odd)
+    )
 
 
 def forward(wave, tables):
-    return along_rows(along_columns(wave, tables.at[0]), tables.at[1])
+    return apart(apart(wave, tables.at[0], 1), tables.at[1], 0)
 
 
 def inverse(wave, tables):
-    return along_rows(along_columns(wave, tables.at[1]), tables.at[0])
+    return together(together(wave, tables.at[1], 1), tables.at[0], 0)
+
+
+def reorder_kernel(image, pick, out):
+    def moved(value, axis):
+        total = None
+        for _ in range(3):
+            term = value.astype(jnp.bfloat16)
+            value = value - term.astype(jnp.float32)
+            term = dot(term, pick[1]) if axis else dot(pick[0], term)
+            total = term if total is None else total + term
+        return total
+
+    out[0] = moved(moved(image[0], 1), 0)
+
+
+def reorder(images):
+    count, window, _ = images.shape
+    order = np.concatenate([np.arange(0, window, 2), np.arange(1, window, 2)])
+    pick = np.eye(window)[order]
+    pick = jnp.asarray(np.stack([pick, pick.T]).astype(ml_dtypes.bfloat16))
+    spec = pl.BlockSpec((1, window, window), lambda image: (image, 0, 0))
+    return pl.pallas_call(
+        reorder_kernel,
+        grid=(count,),
+        in_specs=[spec, whole(pick.shape)],
+        out_specs=spec,
+        out_shape=jax.ShapeDtypeStruct(images.shape, jnp.float32),
+        name="reorder",
+        compiler_params=pltpu.CompilerParams(vmem_limit_bytes=LIMIT),
+        cost_estimate=pl.CostEstimate(
+            flops=count * 12 * window**3, bytes_accessed=8 * images.size, transcendentals=0
+        ),
+    )(images, pick)
 
 
 def product(first, second):
@@ -110,8 +165,8 @@
         bottom = value - top
         for rows, piece in ((block, top), (block + 1, bottom)):
             kept = jnp.where(left, piece, 0.0)
-            total[0, rows, part] += kept
-            total[1, rows, part] += piece - kept
+            total[rows, 0, part] += kept
+            total[rows, 1, part] += piece - kept
 
 
 def shifted(wave, row, column):
@@ -188,9 +243,9 @@
     return pl.BlockSpec(shape, lambda slot: (0,) * len(shape))
 
 
-def call(body, capacity, window, layer, operands, specs, outs, out_specs, name):
+def call(body, capacity, window, layer, operands, specs, outs, out_specs, name, weight=1):
     block = (2, window, window)
-    passes = 2 * 24 * 2 * window**3
+    passes = weight * 2 * 12 * 2 * window**3
     return pl.pallas_call(
         body,
         grid=(capacity,),
@@ -220,26 +275,61 @@
     return lax.ppermute(value, axis, [(source, source + steps) for source in range(leading, last)])
 
 
+def around(value, steps):
+    count = lax.axis_size("col")
+    return lax.ppermute(value, "col", [(i, i // 4 * 4 + (i + steps) % 4) for i in range(count)])
+
+
+def across(value, moved, steps):
+    edge = 3 if steps < 0 else 0
+    count = lax.axis_size("col")
+    pairs = [(i, i + 4 * steps) for i in range(edge, count, 4) if 0 <= i + 4 * steps < count]
+    passed = lax.ppermute(value, "col", pairs)
+    return jnp.where(lax.axis_index("col") % 4 == edge, passed, moved)
+
+
+def after(value, *earlier):
+    for other in earlier:
+        value = value + 0.0 * other[(0,) * other.ndim]
+    return value
+
+
 def exchange(value, axis, bit):
     return lax.ppermute(value, axis, [(i, i ^ bit) for i in range(lax.axis_size(axis))])
 
 
-def sum_everywhere(value):
+def bits(axis, low):
+    place = lax.axis_index(axis)
+    return place & low != 0, place & (2 * low) != 0
+
+
+def ordered(pieces, swaps):
+    for step, swap in zip((1, 2), swaps):
+        pieces = [jnp.where(swap, pieces[k ^ step], pieces[k]) for k in range(len(pieces))]
+    return pieces
+
+
+def sum_everywhere(value, waits):
     shape = value.shape
     value = value.reshape(-1, shape[-1])
-    scattered = (("row", 1), ("col", 1), ("col", 8))
-    whole_sums = (("col", 2), ("col", 16), ("col", 4), ("row", 2), ("row", 4))
-    for axis, bit in scattered:
-        first = lax.axis_index(axis) & bit == 0
-        low, high = jnp.split(value, 2)
-        kept, sent = jnp.where(first, low, high), jnp.where(first, high, low)
-        value = kept + exchange(sent, axis, bit)
-    for axis, bit in whole_sums:
-        value = value + exchange(value, axis, bit)
-    for axis, bit in reversed(scattered):
-        first = lax.axis_index(axis) & bit == 0
-        other = exchange(value, axis, bit)
-        value = jnp.concatenate([jnp.where(first, value, other), jnp.where(first, other, value)])
+    core = lax.axis_index("row") & 1 != 0
+    low, high = jnp.split(value, 2)
+    value = jnp.where(core, high, low) + exchange(jnp.where(core, low, high), "row", 1)
+    value = after(value, *waits[0])
+    swaps = bits("col", 8)
+    parts = ordered(jnp.split(value, 4), swaps)
+    others = [exchange(parts[k], "col", 8 * k) for k in (1, 2, 3)]
+    value = (parts[0] + others[0]) + (others[1] + others[2])
+    for at, (axis, low) in enumerate((("col", 1), ("row", 2))):
+        value = after(value, *waits[at + 1])
+        others = [exchange(value, axis, k * low) for k in (1, 2, 3)]
+        value = (value + others[0]) + (others[1] + others[2])
+    value = value + exchange(value, "col", 4)
+    value = after(value, *waits[3])
+    others = [exchange(value, "col", 8 * k) for k in (1, 2, 3)]
+    value = jnp.concatenate(ordered([value, *others], swaps))
+    other = exchange(value, "row", 1)
+    value = jnp.concatenate([jnp.where(core, other, value), jnp.where(core, value, other)])
     return value.reshape(shape)
 
 
@@ -247,7 +337,8 @@
     window = probe.shape[-1]
     capacity = intensity.shape[2]
     offsets = slot_offset[0, 0]
-    measured = intensity[0, 0]
+    measured = reorder(intensity[0, 0])
+    prop_phase = reorder(prop_phase[None])[0]
     tables = jnp.asarray(dft_blocks(window))
     kernel = jnp.stack([jnp.cos(prop_phase), jnp.sin(prop_phase)])
     block = (2, window, window)
@@ -255,27 +346,35 @@
     per_slot = jax.ShapeDtypeStruct((capacity, *block), f32)
     slot_spec = pl.BlockSpec((1, *block), lambda slot: (slot, 0, 0, 0))
     table_spec = whole(tables.shape)
-    total_shape = (2, 3, *block)
+    total_shape = (3, 2, *block)
     total = jax.ShapeDtypeStruct(total_shape, f32)
 
-    def halo(layer):
-        top, bottom = object_field[layer, :, :window], object_field[layer, :, window:]
+    rows, columns = lax.axis_size("row"), lax.axis_size("col")
+
+    def between(value, move):
+        pairs = []
+        for row in range(rows):
+            for column in range(columns):
+                to_row, to_column = move(row, column)
+                if 0 <= to_row < rows and 0 <= to_column < columns:
+                    pairs.append((row * columns + column, to_row * columns + to_column))
+        return lax.ppermute(value, ("row", "col"), pairs)
+
+    def halo(field):
+        top, bottom = field[:, :, :window], field[:, :, window:]
         right_top = from_behind(top, "col", -1)
         below = from_behind(top, "row", -1)
-        right_bottom = from_behind(bottom, "col", -1)
-        diagonal = from_behind(right_top, "row", -1)
-        return right_top, right_bottom, below, diagonal
-
-    def gather(total):
-        own, right = total[0], total[1]
-        below = from_behind(own[2], "row", 1)
-        diagonal = from_behind(right[2], "row", 1)
-        from_left_top = from_behind(right[0] + diagonal, "col", 1)
-        from_left_bottom = from_behind(right[1], "col", 1)
-        return jnp.concatenate([own[0] + below + from_left_top, own[1] + from_left_bottom], axis=1)
-
-    near = halo(0)
-    far = halo(1)
+        moved = around(bottom, -1)
+        near_corner = between(right_top, lambda r, c: (r - 1 if r % 2 else -1, c))
+        far_corner = between(below, lambda r, c: (r if r % 2 else -1, c - 1))
+        right_bottom = across(moved, moved, -1)
+        return right_top, right_bottom, below, near_corner + far_corner
+
+    def send_down(total):
+        return from_behind(total[2], "row", 1), around(total[1, 1], 1)
+
+    near = tuple(part[0] for part in halo(object_field[:1]))
+    far = tuple(part[0] for part in halo(object_field[1:]))
     first = (slot_count, offsets, object_field)
     arriving = call(
         arrive_kernel, capacity, window, 0,
@@ -293,11 +392,19 @@
         leave_kernel, capacity, window, 0,
         (*first, *near, probe, kernel, leaving, tables),
         (whole(block), whole(block), slot_spec, table_spec),
-        (total, jax.ShapeDtypeStruct(block, f32)), (whole(total_shape), whole(block)), "leave",
-    )
-    last_grad = gather(last_total)
-    first_grad = gather(first_total)
-    probe_grad = sum_everywhere(probe_total)
+        (total, jax.ShapeDtypeStruct(block, f32)), (whole(total_shape), whole(block)), "leave", 8,
+    )
+    def gather(total):
+        down, moved = send_down(total)
+        left_top = from_behind(total[0, 1] + down[1], "col", 1)
+        left_bottom = across(moved, moved, 1)
+        grad = [total[0, 0] + down[0] + left_top, total[1, 0] + left_bottom]
+        return jnp.concatenate(grad, axis=1), (down, moved), (left_top, left_bottom)
+
+    last_grad, last_down, last_over = gather(last_total)
+    first_grad, first_down, first_over = gather(first_total)
+    waits = ((last_down[0],), (first_down[1],), (first_down[0],), last_over)
+    probe_grad = sum_everywhere(after(probe_total, last_down[1]), waits)
     return (jnp.stack([first_grad, last_grad]), probe_grad)
 
 

time: 255 us -> 199 us (0.78)
  the two profiles are of different devices: /device:TPU:34 before, /device:TPU:57 now
where the time goes in v2:
time: 199 us; the launch traced here: 201 us
  starting transfers between devices  102 us (51%)
  waiting for transfers between devices  51.8 us (26%)
  Pallas kernels  18.8 us (9%)
  other arithmetic  12 us (6%)
  local copies, waits for them, and re-layouts  10.6 us (5%)
  between operations  5.96 us (3%)
    ppermute x15, starting transfers between devices, exchange(): lax.ppermute(value, axis, [(i, i ^ bit) for i in range(lax.axis_size(axis...  48.5 us
    ppermute x8, starting transfers between devices, from_behind(): lax.ppermute(value, axis, [(source, source + steps) for source in range(l...  38.8 us
    ppermute x4, waiting for transfers between devices, around(): lax.ppermute(value, 'col', [(i, i // 4 * 4 + (i + steps) % 4) for i in ra...  30.7 us
    pallas_call x3, Pallas kernels, call(): pl.pallas_call(body, grid=(capacity,), in_specs=[pl.BlockSpec(memory_spac...  15.4 us
    ppermute x15, waiting for transfers between devices, exchange(): lax.ppermute(value, axis, [(i, i ^ bit) for i in range(lax.axis_size(axis...  14.5 us
    ppermute x4, starting transfers between devices, between(): return lax.ppermute(value, ('row', 'col'), pairs)  9.01 us
    ppermute x4, starting transfers between devices, across(): passed = lax.ppermute(value, 'col', pairs)  5.21 us
    slice x6, local copies, waits for them, and re-layouts, after(): value = value + 0.0 * other[(0,) * other.ndim]  4.7 us
  transfers between devices with their start and end apart: 35, of which 11 were waited for; matrix products, arithmetic and copies ran while one was open for 9% of the time, Pallas kernels for 7%

profile of v2, /device:TPU:57, one launch (start us, length us, event | category | flops | bytes accessed | tf_op | source)
XLA Modules:
  0.0 201.4 jit_solution(13230995503898144431)
XLA Ops:
  0.7 2.7 %fusion.7 = (f32[1,2,256,256]{3,2,1,0:T(8,128)S(1)}, f32[1,2,256,256]{3,2,1,0:T(8,128)S(1)}, f32[1,2,256,256]{3,2,1,0:T(8,128)}, f32[1,2,256,256]{3,2,1,0:T(8,128)}) fusion(f32[2,2,512,256]{3,2,1,0:T(8,128)} %own.5), kind=kLoop, calls=%fused_computation.52 | loop fusion | bytes 4194304 | tf_op jit(solution)/shard_map/slice | solution.py:364
  3.9 2.1 %collective-permute-start = (f32[1,2,256,256]{3,2,1,0:T(8,128)}, f32[1,2,256,256]{3,2,1,0:T(8,128)S(1)}, u32[]{:S(2)}, u32[]{:S(2)}) collective-permute-start(f32[1,2,256,256]{3,2,1,0:T(8,128)} %get-tuple-element.18), channel_id=1, source_target_pairs={{1,0},{2,1},{3,2},{4,3},{5,4},{6,5},{7,6},{8,7},{9,8},{10,9},{11,1... | collective-permute-start | bytes 1572872 | tf_op jit(solution)/shard_map/ppermute | solution.py:275
  6.2 3.4 %collective-permute-start.3 = (f32[1,2,256,256]{3,2,1,0:T(8,128)}, f32[1,2,256,256]{3,2,1,0:T(8,128)S(1)}, u32[]{:S(2)}, u32[]{:S(2)}) collective-permute-start(f32[1,2,256,256]{3,2,1,0:T(8,128)} %get-tuple-element.18), channel_id=1, source_target_pairs={{32,0},{64,32},{96,64},{128,96},{160,128},{192,160},{224,192},{33,... | collective-permute-start | bytes 1572872 | tf_op jit(solution)/shard_map/ppermute | solution.py:275
  9.6 4.6 %collective-permute-start.6 = (f32[1,2,256,256]{3,2,1,0:T(8,128)}, f32[1,2,256,256]{3,2,1,0:T(8,128)S(1)}, u32[]{:S(2)}, u32[]{:S(2)}) collective-permute-start(f32[1,2,256,256]{3,2,1,0:T(8,128)} %get-tuple-element.17), channel_id=1, source_target_pairs={{1,0},{2,1},{3,2},{4,3},{5,4},{6,5},{7,6},{8,7},{9,8},{10,9},{11,1... | collective-permute-start | bytes 1572872 | tf_op jit(solution)/shard_map/ppermute | solution.py:275
  14.3 25.7 %collective-permute-done.1 = f32[1,2,256,256]{3,2,1,0:T(8,128)} collective-permute-done((f32[1,2,256,256]{3,2,1,0:T(8,128)S(1)}, f32[1,2,256,256]{3,2,1,0:T(8,128)}, u32[]{:S(2)}, u32[]{:S(2)}) %collective-permute-start.1) | collective-permute-done | bytes 524320 | tf_op jit(solution)/shard_map/ppermute | solution.py:280
  40.0 4.6 %collective-permute-start.9 = (f32[1,2,256,256]{3,2,1,0:T(8,128)}, f32[1,2,256,256]{3,2,1,0:T(8,128)}, u32[]{:S(2)}, u32[]{:S(2)}) collective-permute-start(f32[1,2,256,256]{3,2,1,0:T(8,128)} %get-tuple-element.17), channel_id=1, source_target_pairs={{32,0},{64,32},{96,64},{128,96},{160,128},{192,160},{224,192},{33,... | collective-permute-start | bytes 1572872 | tf_op jit(solution)/shard_map/ppermute | solution.py:275
  44.6 1.9 collective-permute-start.2
  47.2 4.0 %collective-permute-done.7 = f32[1,2,256,256]{3,2,1,0:T(8,128)} collective-permute-done((f32[1,2,256,256]{3,2,1,0:T(8,128)S(1)}, f32[1,2,256,256]{3,2,1,0:T(8,128)}, u32[]{:S(2)}, u32[]{:S(2)}) %collective-permute-start.7) | collective-permute-done | bytes 524320 | tf_op jit(solution)/shard_map/ppermute | solution.py:280
  51.2 1.9 collective-permute-start.8
  53.1 1.0 fusion.8
  54.9 2.7 %reorder.3.measured = f32[4,256,256]{2,1,0:T(8,128)S(1)} custom-call(f32[4,256,256]{2,1,0:T(8,128)S(1)} %bitcast.73, bf16[2,256,256]{2,1,0:T(8,128)(2,1)S(1)} %copy-done.3), custom_call_target="tpu_custom_call" | custom-call | flops 805306368 | bytes 2097152 | tf_op jit(solution)/shard_map/reorder/pallas_call | solution.py:103
  57.7 3.8 %collective-permute-start.4 = (f32[1,2,256,256]{3,2,1,0:T(8,128)S(1)}, f32[1,2,256,256]{3,2,1,0:T(8,128)S(1)}, u32[]{:S(2)}, u32[]{:S(2)}) collective-permute-start(f32[1,2,256,256]{3,2,1,0:T(8,128)S(1)} %collective-permute-done), channel_id=1, source_target_pairs={{32,0},{33,1},{34,2},{35,3},{36,4},{37,5},{38,6},{39,7},{40,8},{41... | collective-permute-start | bytes 1572872 | tf_op jit(solution)/shard_map/ppermute | solution.py:361
  61.6 1.9 collective-permute-start.5
  63.5 1.3 collective-permute-start.10
  64.9 1.9 collective-permute-start.11
  66.8 1.1 select_bitcast_fusion.1.right_bottom
  67.9 4.6 %collective-permute-done.8 = f32[1,2,256,256]{3,2,1,0:T(8,128)} collective-permute-done((f32[1,2,256,256]{3,2,1,0:T(8,128)}, f32[1,2,256,256]{3,2,1,0:T(8,128)}, u32[]{:S(2)}, u32[]{:S(2)}) %collective-permute-start.8) | collective-permute-done | bytes 524320 | tf_op jit(solution)/shard_map/ppermute | solution.py:287
  72.6 1.1 select_bitcast_fusion.right_bottom
  74.6 4.4 %arrive.1.arriving = f32[4,2,256,256]{3,2,1,0:T(8,128)S(1)} custom-call(s32[1,1]{1,0:T(1,128)S(6)} %copy.14.count, s32[4,2]{1,0:T(4,128)S(1)} %copy.13.offsets, f32[2,2,512,256]{3,2,1,0:T(8,128)S(1)} %copy-done.1, f32[2,256,256]{2,1,0:T(8,128)S(1)} %bitcast.74, f32[2,256,256]{2,1,0:T(8,128)S(1)} %select_bitcast_fusion.1.right_bottom, ...), custom_call_target="tpu_custom_call" | custom-call | flops 3221225472 | bytes 8388608 | tf_op jit(solution)/shard_map/arrive/pallas_call | solution.py:249
  79.1 1.1 collective-permute-done.11
  80.2 5.5 %misfit.1 = (f32[3,2,2,256,256]{4,3,2,1,0:T(8,128)S(1)}, f32[4,2,256,256]{3,2,1,0:T(8,128)S(1)}) custom-call(s32[1,1]{1,0:T(1,128)S(6)} %copy.14.count, s32[4,2]{1,0:T(4,128)S(1)} %copy.13.offsets, f32[2,2,512,256]{3,2,1,0:T(8,128)S(1)} %copy-done.1, f32[2,256,256]{2,1,0:T(8,128)S(1)} %bitcast.78, f32[2,256,256]{2,1,0:T(8,128)S(1)} %select_bitcast_fusion.right_bottom, ...), custom_call_target="tpu_custom_call" | custom-call | flops 3221225472 | bytes 8388608 | tf_op jit(solution)/shard_map/misfit/pallas_call | solution.py:249
  86.0 2.3 %collective-permute-start.16 = (f32[2,2,256,256]{3,2,1,0:T(8,128)S(1)}, f32[2,2,256,256]{3,2,1,0:T(8,128)S(1)}, u32[]{:S(2)}, u32[]{:S(2)}) collective-permute-start(f32[2,2,256,256]{3,2,1,0:T(8,128)S(1)} %slice_bitcast_fusion), channel_id=1, source_target_pairs={{0,32},{32,64},{64,96},{96,128},{128,160},{160,192},{192,224},{1,3... | collective-permute-start | bytes 3145736 | tf_op jit(solution)/shard_map/ppermute | solution.py:275
  88.4 5.6 %leave.1 = (f32[3,2,2,256,256]{4,3,2,1,0:T(8,128)S(1)}, f32[2,256,256]{2,1,0:T(8,128)S(1)}) custom-call(s32[1,1]{1,0:T(1,128)S(6)} %copy.14.count, s32[4,2]{1,0:T(4,128)S(1)} %copy.13.offsets, f32[2,2,512,256]{3,2,1,0:T(8,128)S(1)} %copy-done.1, f32[2,256,256]{2,1,0:T(8,128)S(1)} %bitcast.75, f32[2,256,256]{2,1,0:T(8,128)S(1)} %select_bitcast_fusion.1.right_bottom, ...), custom_call_target="tpu_custom_call" | custom-call | flops 25769803776 | bytes 8388608 | tf_op jit(solution)/shard_map/leave/pallas_call | solution.py:249
  93.9 1.0 collective-permute-done.18
  96.3 1.0 slice_bitcast_fusion.1
  97.4 17.1 %collective-permute-start.12 = (f32[2,2,256,256]{3,2,1,0:T(8,128)}, f32[2,2,256,256]{3,2,1,0:T(8,128)}, u32[]{:S(2)}, u32[]{:S(2)}) collective-permute-start(f32[2,2,256,256]{3,2,1,0:T(8,128)} %slice_bitcast_fusion.1), channel_id=1, source_target_pairs={{0,32},{32,64},{64,96},{96,128},{128,160},{160,192},{192,224},{1,3... | collective-permute-start | bytes 3145736 | tf_op jit(solution)/shard_map/ppermute | solution.py:275
  117.4 1.1 collective-permute-start.21
  118.5 15.1 %collective-permute-start.22 = (f32[64,256]{1,0:T(8,128)}, f32[64,256]{1,0:T(8,128)}, u32[]{:S(2)}, u32[]{:S(2)}) collective-permute-start(f32[64,256]{1,0:T(8,128)} %get-tuple-element.26), channel_id=1, source_target_pairs={{0,16},{1,17},{2,18},{3,19},{4,20},{5,21},{6,22},{7,23},{8,24},{9,... | collective-permute-start | bytes 196616 | tf_op jit(solution)/shard_map/ppermute | solution.py:298
  133.6 1.3 slice.110
  136.3 1.7 collective-permute-done.23
  138.0 0.9 add_add_fusion.3
  138.9 1.4 collective-permute-start.24
  140.3 2.5 %collective-permute-start.26 = (f32[64,256]{1,0:T(8,128)S(1)}, f32[64,256]{1,0:T(8,128)S(1)}, u32[]{:S(2)}, u32[]{:S(2)}) collective-permute-start(f32[64,256]{1,0:T(8,128)S(1)} %add_add_fusion.3), channel_id=1, source_target_pairs={{0,3},{1,2},{2,1},{3,0},{4,7},{5,6},{6,5},{7,4},{8,11},{9,10},{10,... | collective-permute-start | bytes 196616 | tf_op jit(solution)/shard_map/ppermute | solution.py:298
  142.9 1.3 fusion
  144.2 1.2 slice.111
  146.0 2.7 %collective-permute-start.17 = (f32[2,256,256]{2,1,0:T(8,128)S(1)}, f32[2,256,256]{2,1,0:T(8,128)S(1)}, u32[]{:S(2)}, u32[]{:S(2)}) collective-permute-start(f32[2,256,256]{2,1,0:T(8,128)S(1)} %fusion), channel_id=1, source_target_pairs={{0,1},{1,2},{2,3},{3,4},{4,5},{5,6},{6,7},{7,8},{8,9},{9,10},{10,1... | collective-permute-start | bytes 1572872 | tf_op jit(solution)/shard_map/ppermute | solution.py:275
  148.7 8.9 %collective-permute-start.27 = (f32[64,256]{1,0:T(8,128)S(1)}, f32[64,256]{1,0:T(8,128)S(1)}, u32[]{:S(2)}, u32[]{:S(2)}) collective-permute-start(f32[64,256]{1,0:T(8,128)S(1)} %add_add_fusion.2), channel_id=1, source_target_pairs={{0,64},{32,96},{64,0},{96,32},{128,192},{160,224},{192,128},{224,1... | collective-permute-start | bytes 196616 | tf_op jit(solution)/shard_map/ppermute | solution.py:298
  157.6 3.4 %collective-permute-start.29 = (f32[64,256]{1,0:T(8,128)S(1)}, f32[64,256]{1,0:T(8,128)S(1)}, u32[]{:S(2)}, u32[]{:S(2)}) collective-permute-start(f32[64,256]{1,0:T(8,128)S(1)} %add_add_fusion.2), channel_id=1, source_target_pairs={{0,192},{32,224},{64,128},{96,160},{128,64},{160,96},{192,0},{224,... | collective-permute-start | bytes 196616 | tf_op jit(solution)/shard_map/ppermute | solution.py:298
  161.0 1.1 fusion.3
  162.1 8.2 %collective-permute-done.27 = f32[64,256]{1,0:T(8,128)S(1)} collective-permute-done((f32[64,256]{1,0:T(8,128)S(1)}, f32[64,256]{1,0:T(8,128)S(1)}, u32[]{:S(2)}, u32[]{:S(2)}) %collective-permute-start.27) | collective-permute-done | bytes 65568 | tf_op jit(solution)/shard_map/ppermute | solution.py:298
  171.0 1.9 collective-permute-start.13
  173.1 1.4 bitcast_add_fusion
  176.9 2.9 %collective-permute-done.30 = f32[64,256]{1,0:T(8,128)S(1)} collective-permute-done((f32[64,256]{1,0:T(8,128)S(1)}, f32[64,256]{1,0:T(8,128)S(1)}, u32[]{:S(2)}, u32[]{:S(2)}) %collective-permute-start.30) | collective-permute-done | bytes 65568 | tf_op jit(solution)/shard_map/ppermute | solution.py:298
  179.9 7.7 %collective-permute-start.32 = (f32[64,256]{1,0:T(8,128)S(1)}, f32[64,256]{1,0:T(8,128)S(1)}, u32[]{:S(2)}, u32[]{:S(2)}) collective-permute-start(f32[64,256]{1,0:T(8,128)S(1)} %add_add_fusion), channel_id=1, source_target_pairs={{0,16},{1,17},{2,18},{3,19},{4,20},{5,21},{6,22},{7,23},{8,24},{9,... | collective-permute-start | bytes 196616 | tf_op jit(solution)/shard_map/ppermute | solution.py:298
  187.6 1.4 fusion.5
  189.2 1.5 collective-permute-done.33
  190.8 8.1 %collective-permute-start.34 = (f32[256,256]{1,0:T(8,128)S(1)}, f32[256,256]{1,0:T(8,128)S(1)}, u32[]{:S(2)}, u32[]{:S(2)}) collective-permute-start(f32[256,256]{1,0:T(8,128)S(1)} %pad_maximum_fusion.3), channel_id=1, source_target_pairs={{0,32},{32,0},{64,96},{96,64},{128,160},{160,128},{192,224},{224,1... | collective-permute-start | bytes 786440 | tf_op jit(solution)/shard_map/ppermute | solution.py:298
  199.0 1.5 pad_maximum_fusion
  (95 shorter events, 9.6 us)
Async XLA Ops:
  0.6 45.9 %copy-start.3 = (bf16[2,256,256]{2,1,0:T(8,128)(2,1)S(1)}, bf16[2,256,256]{2,1,0:T(8,128)(2,1)}, u32[]{:S(2)}) copy-start(bf16[2,256,256]{2,1,0:T(8,128)(2,1)} %constant.49.clone.pick) | copy-start | bytes 786436
  0.6 45.9 %copy-start.2 = (f32[256,256]{1,0:T(8,128)S(1)}, f32[256,256]{1,0:T(8,128)}, u32[]{:S(2)}) copy-start(f32[256,256]{1,0:T(8,128)} %param.11) | copy-start | bytes 786436
  0.7 53.5 %copy-start.15 = (s32[1,1,4,2]{2,3,1,0:T(2,128)S(1)}, s32[1,1,4,2]{2,3,1,0:T(2,128)}, u32[]{:S(2)}) copy-start(s32[1,1,4,2]{2,3,1,0:T(2,128)} %param.13) | copy-start | bytes 100
  0.7 54.2 %copy-start.4 = (f32[1,1,4,256,256]{4,3,2,1,0:T(8,128)S(1)}, f32[1,1,4,256,256]{4,3,2,1,0:T(8,128)}, u32[]{:S(2)}) copy-start(f32[1,1,4,256,256]{4,3,2,1,0:T(8,128)} %param.14) | copy-start | bytes 3145732
  3.4 36.6 %collective-permute-start.1 = (f32[1,2,256,256]{3,2,1,0:T(8,128)S(1)}, f32[1,2,256,256]{3,2,1,0:T(8,128)}, u32[]{:S(2)}, u32[]{:S(2)}) collective-permute-start(f32[1,2,256,256]{3,2,1,0:T(8,128)S(1)} %get-tuple-element.15), channel_id=1, source_target_pairs={{0,3},{1,0},{2,1},{3,2},{4,7},{5,4},{6,5},{7,6},{8,11},{9,8},{10,9... | collective-permute-start | bytes 1572872 | tf_op jit(solution)/shard_map/ppermute | solution.py:280
  3.9 40.7 %collective-permute-start = (f32[1,2,256,256]{3,2,1,0:T(8,128)}, f32[1,2,256,256]{3,2,1,0:T(8,128)S(1)}, u32[]{:S(2)}, u32[]{:S(2)}) collective-permute-start(f32[1,2,256,256]{3,2,1,0:T(8,128)} %get-tuple-element.18), channel_id=1, source_target_pairs={{1,0},{2,1},{3,2},{4,3},{5,4},{6,5},{7,6},{8,7},{9,8},{10,9},{11,1... | collective-permute-start | bytes 1572872 | tf_op jit(solution)/shard_map/ppermute | solution.py:275
  5.9 45.3 %collective-permute-start.7 = (f32[1,2,256,256]{3,2,1,0:T(8,128)S(1)}, f32[1,2,256,256]{3,2,1,0:T(8,128)}, u32[]{:S(2)}, u32[]{:S(2)}) collective-permute-start(f32[1,2,256,256]{3,2,1,0:T(8,128)S(1)} %get-tuple-element.16), channel_id=1, source_target_pairs={{0,3},{1,0},{2,1},{3,2},{4,7},{5,4},{6,5},{7,6},{8,11},{9,8},{10,9... | collective-permute-start | bytes 1572872 | tf_op jit(solution)/shard_map/ppermute | solution.py:280
  6.2 51.5 %collective-permute-start.3 = (f32[1,2,256,256]{3,2,1,0:T(8,128)}, f32[1,2,256,256]{3,2,1,0:T(8,128)S(1)}, u32[]{:S(2)}, u32[]{:S(2)}) collective-permute-start(f32[1,2,256,256]{3,2,1,0:T(8,128)} %get-tuple-element.18), channel_id=1, source_target_pairs={{32,0},{64,32},{96,64},{128,96},{160,128},{192,160},{224,192},{33,... | collective-permute-start | bytes 1572872 | tf_op jit(solution)/shard_map/ppermute | solution.py:275
  9.6 52.0 %collective-permute-start.6 = (f32[1,2,256,256]{3,2,1,0:T(8,128)}, f32[1,2,256,256]{3,2,1,0:T(8,128)S(1)}, u32[]{:S(2)}, u32[]{:S(2)}) collective-permute-start(f32[1,2,256,256]{3,2,1,0:T(8,128)} %get-tuple-element.17), channel_id=1, source_target_pairs={{1,0},{2,1},{3,2},{4,3},{5,4},{6,5},{7,6},{8,7},{9,8},{10,9},{11,1... | collective-permute-start | bytes 1572872 | tf_op jit(solution)/shard_map/ppermute | solution.py:275
  40.0 23.5 %collective-permute-start.9 = (f32[1,2,256,256]{3,2,1,0:T(8,128)}, f32[1,2,256,256]{3,2,1,0:T(8,128)}, u32[]{:S(2)}, u32[]{:S(2)}) collective-permute-start(f32[1,2,256,256]{3,2,1,0:T(8,128)} %get-tuple-element.17), channel_id=1, source_target_pairs={{32,0},{64,32},{96,64},{128,96},{160,128},{192,160},{224,192},{33,... | collective-permute-start | bytes 1572872 | tf_op jit(solution)/shard_map/ppermute | solution.py:275
  44.6 30.0 %copy-start.6 = (f32[1,2,256,256]{3,2,1,0:T(8,128)}, f32[1,2,256,256]{3,2,1,0:T(8,128)S(1)}, u32[]{:S(2)}) copy-start(f32[1,2,256,256]{3,2,1,0:T(8,128)S(1)} %collective-permute-done) | copy-start | bytes 1572868
  44.6 20.3 %collective-permute-start.2 = (f32[1,2,256,256]{3,2,1,0:T(8,128)}, f32[1,2,256,256]{3,2,1,0:T(8,128)}, u32[]{:S(2)}, u32[]{:S(2)}) collective-permute-start(f32[1,2,256,256]{3,2,1,0:T(8,128)} %collective-permute-done.1), channel_id=1, source_target_pairs={{7,3},{11,7},{15,11},{19,15},{23,19},{27,23},{31,27},{39,35},{43,3... | collective-permute-start | bytes 1572872 | tf_op jit(solution)/shard_map/ppermute | solution.py:287
  51.2 21.4 %collective-permute-start.8 = (f32[1,2,256,256]{3,2,1,0:T(8,128)}, f32[1,2,256,256]{3,2,1,0:T(8,128)}, u32[]{:S(2)}, u32[]{:S(2)}) collective-permute-start(f32[1,2,256,256]{3,2,1,0:T(8,128)} %collective-permute-done.7), channel_id=1, source_target_pairs={{7,3},{11,7},{15,11},{19,15},{23,19},{27,23},{31,27},{39,35},{43,3... | collective-permute-start | bytes 1572872 | tf_op jit(solution)/shard_map/ppermute | solution.py:287
  57.6 17.0 %copy-start.1 = (f32[2,2,512,256]{3,2,1,0:T(8,128)S(1)}, f32[2,2,512,256]{3,2,1,0:T(8,128)}, u32[]{:S(2)}) copy-start(f32[2,2,512,256]{3,2,1,0:T(8,128)} %own.5) | copy-start | bytes 6291460
  57.7 17.0 %copy-start.5 = (f32[2,256,256]{2,1,0:T(8,128)S(1)}, f32[2,256,256]{2,1,0:T(8,128)}, u32[]{:S(2)}) copy-start(f32[2,256,256]{2,1,0:T(8,128)} %probe.3) | copy-start | bytes 1572868
  57.7 17.0 %copy-start.10 = (bf16[2,2,2,256,256]{4,3,2,1,0:T(8,128)(2,1)S(1)}, bf16[2,2,2,256,256]{4,3,2,1,0:T(8,128)(2,1)}, u32[]{:S(2)}) copy-start(bf16[2,2,2,256,256]{4,3,2,1,0:T(8,128)(2,1)} %constant.50.clone.tables) | copy-start | bytes 3145732
  57.7 21.3 %copy-start.8 = (f32[1,2,256,256]{3,2,1,0:T(8,128)}, f32[1,2,256,256]{3,2,1,0:T(8,128)S(1)}, u32[]{:S(2)}) copy-start(f32[1,2,256,256]{3,2,1,0:T(8,128)S(1)} %collective-permute-done.3) | copy-start | bytes 1572868
  57.7 16.0 %collective-permute-start.4 = (f32[1,2,256,256]{3,2,1,0:T(8,128)S(1)}, f32[1,2,256,256]{3,2,1,0:T(8,128)S(1)}, u32[]{:S(2)}, u32[]{:S(2)}) collective-permute-start(f32[1,2,256,256]{3,2,1,0:T(8,128)S(1)} %collective-permute-done), channel_id=1, source_target_pairs={{32,0},{33,1},{34,2},{35,3},{36,4},{37,5},{38,6},{39,7},{40,8},{41... | collective-permute-start | bytes 1572872 | tf_op jit(solution)/shard_map/ppermute | solution.py:361
  61.6 12.9 %collective-permute-start.5 = (f32[1,2,256,256]{3,2,1,0:T(8,128)S(1)}, f32[1,2,256,256]{3,2,1,0:T(8,128)S(1)}, u32[]{:S(2)}, u32[]{:S(2)}) collective-permute-start(f32[1,2,256,256]{3,2,1,0:T(8,128)S(1)} %collective-permute-done.3), channel_id=1, source_target_pairs={{33,32},{34,33},{35,34},{36,35},{37,36},{38,37},{39,38},{40,39},{4... | collective-permute-start | bytes 1572872 | tf_op jit(solution)/shard_map/ppermute | solution.py:361
  63.5 15.5 %collective-permute-start.10 = (f32[1,2,256,256]{3,2,1,0:T(8,128)S(1)}, f32[1,2,256,256]{3,2,1,0:T(8,128)S(1)}, u32[]{:S(2)}, u32[]{:S(2)}) collective-permute-start(f32[1,2,256,256]{3,2,1,0:T(8,128)S(1)} %collective-permute-done.6), channel_id=1, source_target_pairs={{32,0},{33,1},{34,2},{35,3},{36,4},{37,5},{38,6},{39,7},{40,8},{41... | collective-permute-start | bytes 1572872 | tf_op jit(solution)/shard_map/ppermute | solution.py:361
  64.9 15.3 %collective-permute-start.11 = (f32[1,2,256,256]{3,2,1,0:T(8,128)}, f32[1,2,256,256]{3,2,1,0:T(8,128)S(1)}, u32[]{:S(2)}, u32[]{:S(2)}) collective-permute-start(f32[1,2,256,256]{3,2,1,0:T(8,128)} %collective-permute-done.9), channel_id=1, source_target_pairs={{33,32},{34,33},{35,34},{36,35},{37,36},{38,37},{39,38},{40,39},{4... | collective-permute-start | bytes 1572872 | tf_op jit(solution)/shard_map/ppermute | solution.py:361
  85.7 2.6 %copy-start = (f32[3,2,2,256,256]{4,3,2,1,0:T(8,128)}, f32[3,2,2,256,256]{4,3,2,1,0:T(8,128)S(1)}, u32[]{:S(2)}) copy-start(f32[3,2,2,256,256]{4,3,2,1,0:T(8,128)S(1)} %get-tuple-element.8) | copy-start | bytes 9437188
  85.9 9.0 %collective-permute-start.18 = (f32[2,256,256]{2,1,0:T(8,128)S(1)}, f32[2,256,256]{2,1,0:T(8,128)S(1)}, u32[]{:S(2)}, u32[]{:S(2)}) collective-permute-start(f32[2,256,256]{2,1,0:T(8,128)S(1)} %slice_bitcast_fusion.6), channel_id=1, source_target_pairs={{0,1},{1,2},{2,3},{3,0},{4,5},{5,6},{6,7},{7,4},{8,9},{9,10},{10,1... | collective-permute-start | bytes 1572872 | tf_op jit(solution)/shard_map/ppermute | solution.py:280
  86.0 29.4 %collective-permute-start.16 = (f32[2,2,256,256]{3,2,1,0:T(8,128)S(1)}, f32[2,2,256,256]{3,2,1,0:T(8,128)S(1)}, u32[]{:S(2)}, u32[]{:S(2)}) collective-permute-start(f32[2,2,256,256]{3,2,1,0:T(8,128)S(1)} %slice_bitcast_fusion), channel_id=1, source_target_pairs={{0,32},{32,64},{64,96},{96,128},{128,160},{160,192},{192,224},{1,3... | collective-permute-start | bytes 3145736 | tf_op jit(solution)/shard_map/ppermute | solution.py:275
  94.9 22.5 %copy-start.13 = (f32[2,256,256]{2,1,0:T(8,128)}, f32[2,256,256]{2,1,0:T(8,128)S(1)}, u32[]{:S(2)}) copy-start(f32[2,256,256]{2,1,0:T(8,128)S(1)} %collective-permute-done.18) | copy-start | bytes 1572868
  96.2 20.5 %collective-permute-start.20 = (f32[256,256]{1,0:T(8,128)S(1)}, f32[256,256]{1,0:T(8,128)S(1)}, u32[]{:S(2)}, u32[]{:S(2)}) collective-permute-start(f32[256,256]{1,0:T(8,128)S(1)} %select_bitcast_fusion.2), channel_id=1, source_target_pairs={{0,32},{32,0},{64,96},{96,64},{128,160},{160,128},{192,224},{224,1... | collective-permute-start | bytes 786440 | tf_op jit(solution)/shard_map/ppermute | solution.py:298
  97.4 46.8 %collective-permute-start.12 = (f32[2,2,256,256]{3,2,1,0:T(8,128)}, f32[2,2,256,256]{3,2,1,0:T(8,128)}, u32[]{:S(2)}, u32[]{:S(2)}) collective-permute-start(f32[2,2,256,256]{3,2,1,0:T(8,128)} %slice_bitcast_fusion.1), channel_id=1, source_target_pairs={{0,32},{32,64},{64,96},{96,128},{128,160},{160,192},{192,224},{1,3... | collective-permute-start | bytes 3145736 | tf_op jit(solution)/shard_map/ppermute | solution.py:275
  115.3 18.3 %collective-permute-start.14 = (f32[2,256,256]{2,1,0:T(8,128)}, f32[2,256,256]{2,1,0:T(8,128)}, u32[]{:S(2)}, u32[]{:S(2)}) collective-permute-start(f32[2,256,256]{2,1,0:T(8,128)} %slice_bitcast_fusion.7), channel_id=1, source_target_pairs={{0,1},{1,2},{2,3},{3,0},{4,5},{5,6},{6,7},{7,4},{8,9},{9,10},{10,1... | collective-permute-start | bytes 1572872 | tf_op jit(solution)/shard_map/ppermute | solution.py:280
  117.4 18.8 %collective-permute-start.21 = (f32[64,256]{1,0:T(8,128)}, f32[64,256]{1,0:T(8,128)S(1)}, u32[]{:S(2)}, u32[]{:S(2)}) collective-permute-start(f32[64,256]{1,0:T(8,128)} %get-tuple-element.25), channel_id=1, source_target_pairs={{0,8},{1,9},{2,10},{3,11},{4,12},{5,13},{6,14},{7,15},{8,0},{9,1},... | collective-permute-start | bytes 196616 | tf_op jit(solution)/shard_map/ppermute | solution.py:298
  118.5 17.7 %collective-permute-start.22 = (f32[64,256]{1,0:T(8,128)}, f32[64,256]{1,0:T(8,128)}, u32[]{:S(2)}, u32[]{:S(2)}) collective-permute-start(f32[64,256]{1,0:T(8,128)} %get-tuple-element.26), channel_id=1, source_target_pairs={{0,16},{1,17},{2,18},{3,19},{4,20},{5,21},{6,22},{7,23},{8,24},{9,... | collective-permute-start | bytes 196616 | tf_op jit(solution)/shard_map/ppermute | solution.py:298
  133.6 4.4 %collective-permute-start.23 = (f32[64,256]{1,0:T(8,128)S(1)}, f32[64,256]{1,0:T(8,128)}, u32[]{:S(2)}, u32[]{:S(2)}) collective-permute-start(f32[64,256]{1,0:T(8,128)S(1)} %get-tuple-element.27), channel_id=1, source_target_pairs={{0,24},{1,25},{2,26},{3,27},{4,28},{5,29},{6,30},{7,31},{8,16},{9,... | collective-permute-start | bytes 196616 | tf_op jit(solution)/shard_map/ppermute | solution.py:298
  133.6 39.5 %copy-start.12 = (f32[2,2,256,256]{3,2,1,0:T(8,128)S(1)}, f32[2,2,256,256]{3,2,1,0:T(8,128)}, u32[]{:S(2)}) copy-start(f32[2,2,256,256]{3,2,1,0:T(8,128)} %copy-done.11) | copy-start | bytes 3145732
  133.6 39.5 %copy-start.14 = (f32[2,256,256]{2,1,0:T(8,128)S(1)}, f32[2,256,256]{2,1,0:T(8,128)}, u32[]{:S(2)}) copy-start(f32[2,256,256]{2,1,0:T(8,128)} %copy-done.13) | copy-start | bytes 1572868
  135.6 37.5 %collective-permute-start.19 = (f32[2,256,256]{2,1,0:T(8,128)}, f32[2,256,256]{2,1,0:T(8,128)S(1)}, u32[]{:S(2)}, u32[]{:S(2)}) collective-permute-start(f32[2,256,256]{2,1,0:T(8,128)} %copy-done.13), channel_id=1, source_target_pairs={{0,4},{4,8},{8,12},{12,16},{16,20},{20,24},{24,28},{32,36},{36,40}... | collective-permute-start | bytes 1572872 | tf_op jit(solution)/shard_map/ppermute | solution.py:287
  138.9 9.8 %collective-permute-start.24 = (f32[64,256]{1,0:T(8,128)S(1)}, f32[64,256]{1,0:T(8,128)S(1)}, u32[]{:S(2)}, u32[]{:S(2)}) collective-permute-start(f32[64,256]{1,0:T(8,128)S(1)} %add_add_fusion.3), channel_id=1, source_target_pairs={{0,1},{1,0},{2,3},{3,2},{4,5},{5,4},{6,7},{7,6},{8,9},{9,8},{10,11... | collective-permute-start | bytes 196616 | tf_op jit(solution)/shard_map/ppermute | solution.py:298
  140.3 8.4 %collective-permute-start.25 = (f32[64,256]{1,0:T(8,128)S(1)}, f32[64,256]{1,0:T(8,128)S(1)}, u32[]{:S(2)}, u32[]{:S(2)}) collective-permute-start(f32[64,256]{1,0:T(8,128)S(1)} %add_add_fusion.3), channel_id=1, source_target_pairs={{0,2},{1,3},{2,0},{3,1},{4,6},{5,7},{6,4},{7,5},{8,10},{9,11},{10,... | collective-permute-start | bytes 196616 | tf_op jit(solution)/shard_map/ppermute | solution.py:298
  140.3 8.4 %collective-permute-start.26 = (f32[64,256]{1,0:T(8,128)S(1)}, f32[64,256]{1,0:T(8,128)S(1)}, u32[]{:S(2)}, u32[]{:S(2)}) collective-permute-start(f32[64,256]{1,0:T(8,128)S(1)} %add_add_fusion.3), channel_id=1, source_target_pairs={{0,3},{1,2},{2,1},{3,0},{4,7},{5,6},{6,5},{7,4},{8,11},{9,10},{10,... | collective-permute-start | bytes 196616 | tf_op jit(solution)/shard_map/ppermute | solution.py:298
  146.0 27.1 %collective-permute-start.17 = (f32[2,256,256]{2,1,0:T(8,128)S(1)}, f32[2,256,256]{2,1,0:T(8,128)S(1)}, u32[]{:S(2)}, u32[]{:S(2)}) collective-permute-start(f32[2,256,256]{2,1,0:T(8,128)S(1)} %fusion), channel_id=1, source_target_pairs={{0,1},{1,2},{2,3},{3,4},{4,5},{5,6},{6,7},{7,8},{8,9},{9,10},{10,1... | collective-permute-start | bytes 1572872 | tf_op jit(solution)/shard_map/ppermute | solution.py:275
  148.7 21.6 %collective-permute-start.27 = (f32[64,256]{1,0:T(8,128)S(1)}, f32[64,256]{1,0:T(8,128)S(1)}, u32[]{:S(2)}, u32[]{:S(2)}) collective-permute-start(f32[64,256]{1,0:T(8,128)S(1)} %add_add_fusion.2), channel_id=1, source_target_pairs={{0,64},{32,96},{64,0},{96,32},{128,192},{160,224},{192,128},{224,1... | collective-permute-start | bytes 196616 | tf_op jit(solution)/shard_map/ppermute | solution.py:298
  157.6 13.4 %collective-permute-start.28 = (f32[64,256]{1,0:T(8,128)S(1)}, f32[64,256]{1,0:T(8,128)S(1)}, u32[]{:S(2)}, u32[]{:S(2)}) collective-permute-start(f32[64,256]{1,0:T(8,128)S(1)} %add_add_fusion.2), channel_id=1, source_target_pairs={{0,128},{32,160},{64,192},{96,224},{128,0},{160,32},{192,64},{224,... | collective-permute-start | bytes 196616 | tf_op jit(solution)/shard_map/ppermute | solution.py:298
  157.6 15.4 %collective-permute-start.29 = (f32[64,256]{1,0:T(8,128)S(1)}, f32[64,256]{1,0:T(8,128)S(1)}, u32[]{:S(2)}, u32[]{:S(2)}) collective-permute-start(f32[64,256]{1,0:T(8,128)S(1)} %add_add_fusion.2), channel_id=1, source_target_pairs={{0,192},{32,224},{64,128},{96,160},{128,64},{160,96},{192,0},{224,... | collective-permute-start | bytes 196616 | tf_op jit(solution)/shard_map/ppermute | solution.py:298
  170.3 17.2 %collective-permute-start.15 = (f32[2,256,256]{2,1,0:T(8,128)}, f32[2,256,256]{2,1,0:T(8,128)S(1)}, u32[]{:S(2)}, u32[]{:S(2)}) collective-permute-start(f32[2,256,256]{2,1,0:T(8,128)} %collective-permute-done.14), channel_id=1, source_target_pairs={{0,4},{4,8},{8,12},{12,16},{16,20},{20,24},{24,28},{32,36},{36,40}... | collective-permute-start | bytes 1572872 | tf_op jit(solution)/shard_map/ppermute | solution.py:287
  171.0 16.6 %collective-permute-start.13 = (f32[2,256,256]{2,1,0:T(8,128)S(1)}, f32[2,256,256]{2,1,0:T(8,128)S(1)}, u32[]{:S(2)}, u32[]{:S(2)}) collective-permute-start(f32[2,256,256]{2,1,0:T(8,128)S(1)} %fusion.3), channel_id=1, source_target_pairs={{0,1},{1,2},{2,3},{3,4},{4,5},{5,6},{6,7},{7,8},{8,9},{9,10},{10,1... | collective-permute-start | bytes 1572872 | tf_op jit(solution)/shard_map/ppermute | solution.py:275
  173.0 6.8 %collective-permute-start.30 = (f32[64,256]{1,0:T(8,128)S(1)}, f32[64,256]{1,0:T(8,128)S(1)}, u32[]{:S(2)}, u32[]{:S(2)}) collective-permute-start(f32[64,256]{1,0:T(8,128)S(1)} %add_add_fusion.1), channel_id=1, source_target_pairs={{0,4},{1,5},{2,6},{3,7},{4,0},{5,1},{6,2},{7,3},{8,12},{9,13},{10,... | collective-permute-start | bytes 196616 | tf_op jit(solution)/shard_map/ppermute | solution.py:298
  179.8 9.3 %collective-permute-start.31 = (f32[64,256]{1,0:T(8,128)S(1)}, f32[64,256]{1,0:T(8,128)S(1)}, u32[]{:S(2)}, u32[]{:S(2)}) collective-permute-start(f32[64,256]{1,0:T(8,128)S(1)} %add_add_fusion), channel_id=1, source_target_pairs={{0,24},{1,25},{2,26},{3,27},{4,28},{5,29},{6,30},{7,31},{8,16},{9,... | collective-permute-start | bytes 196616 | tf_op jit(solution)/shard_map/ppermute | solution.py:298
  179.9 9.3 %collective-permute-start.32 = (f32[64,256]{1,0:T(8,128)S(1)}, f32[64,256]{1,0:T(8,128)S(1)}, u32[]{:S(2)}, u32[]{:S(2)}) collective-permute-start(f32[64,256]{1,0:T(8,128)S(1)} %add_add_fusion), channel_id=1, source_target_pairs={{0,16},{1,17},{2,18},{3,19},{4,20},{5,21},{6,22},{7,23},{8,24},{9,... | collective-permute-start | bytes 196616 | tf_op jit(solution)/shard_map/ppermute | solution.py:298
  187.6 3.1 %collective-permute-start.33 = (f32[64,256]{1,0:T(8,128)S(1)}, f32[64,256]{1,0:T(8,128)S(1)}, u32[]{:S(2)}, u32[]{:S(2)}) collective-permute-start(f32[64,256]{1,0:T(8,128)S(1)} %add_add_fusion), channel_id=1, source_target_pairs={{0,8},{1,9},{2,10},{3,11},{4,12},{5,13},{6,14},{7,15},{8,0},{9,1},... | collective-permute-start | bytes 196616 | tf_op jit(solution)/shard_map/ppermute | solution.py:298
  190.8 9.8 %collective-permute-start.34 = (f32[256,256]{1,0:T(8,128)S(1)}, f32[256,256]{1,0:T(8,128)S(1)}, u32[]{:S(2)}, u32[]{:S(2)}) collective-permute-start(f32[256,256]{1,0:T(8,128)S(1)} %pad_maximum_fusion.3), channel_id=1, source_target_pairs={{0,32},{32,0},{64,96},{96,64},{128,160},{160,128},{192,224},{224,1... | collective-permute-start | bytes 786440 | tf_op jit(solution)/shard_map/ppermute | solution.py:298
  (3 other events, 6.6 us)

commit v3 on v2

--- a/solution.py
+++ b/solution.py
@@ -290,7 +290,8 @@
 
 def after(value, *earlier):
     for other in earlier:
-        value = value + 0.0 * other[(0,) * other.ndim]
+        other = other.reshape(-1, other.shape[-1])
+        value = value + 0.0 * other[: value.shape[0]]
     return value
 
 
@@ -309,23 +310,27 @@
     return pieces
 
 
-def sum_everywhere(value, waits):
-    shape = value.shape
-    value = value.reshape(-1, shape[-1])
+def sum_chip(value, *earlier):
+    value = after(value.reshape(-1, value.shape[-1]), *earlier)
     core = lax.axis_index("row") & 1 != 0
     low, high = jnp.split(value, 2)
-    value = jnp.where(core, high, low) + exchange(jnp.where(core, low, high), "row", 1)
-    value = after(value, *waits[0])
+    return jnp.where(core, high, low) + exchange(jnp.where(core, low, high), "row", 1)
+
+
+def sum_everywhere(value, shape, waits):
+    core = lax.axis_index("row") & 1 != 0
+    value = after(value, *waits[1])
     swaps = bits("col", 8)
     parts = ordered(jnp.split(value, 4), swaps)
     others = [exchange(parts[k], "col", 8 * k) for k in (1, 2, 3)]
     value = (parts[0] + others[0]) + (others[1] + others[2])
     for at, (axis, low) in enumerate((("col", 1), ("row", 2))):
-        value = after(value, *waits[at + 1])
+        value = after(value, *waits[at + 2])
         others = [exchange(value, axis, k * low) for k in (1, 2, 3)]
         value = (value + others[0]) + (others[1] + others[2])
+    value = after(value, *waits[4])
     value = value + exchange(value, "col", 4)
-    value = after(value, *waits[3])
+    value = after(value, *waits[5])
     others = [exchange(value, "col", 8 * k) for k in (1, 2, 3)]
     value = jnp.concatenate(ordered([value, *others], swaps))
     other = exchange(value, "row", 1)
@@ -394,17 +399,19 @@
         (whole(block), whole(block), slot_spec, table_spec),
         (total, jax.ShapeDtypeStruct(block, f32)), (whole(total_shape), whole(block)), "leave", 8,
     )
-    def gather(total):
-        down, moved = send_down(total)
-        left_top = from_behind(total[0, 1] + down[1], "col", 1)
+    def finish(total, below, moved):
+        left_top = from_behind(total[0, 1] + below[1], "col", 1)
         left_bottom = across(moved, moved, 1)
-        grad = [total[0, 0] + down[0] + left_top, total[1, 0] + left_bottom]
-        return jnp.concatenate(grad, axis=1), (down, moved), (left_top, left_bottom)
-
-    last_grad, last_down, last_over = gather(last_total)
-    first_grad, first_down, first_over = gather(first_total)
-    waits = ((last_down[0],), (first_down[1],), (first_down[0],), last_over)
-    probe_grad = sum_everywhere(after(probe_total, last_down[1]), waits)
+        grad = [total[0, 0] + below[0] + left_top, total[1, 0] + left_bottom]
+        return jnp.concatenate(grad, axis=1), (left_top, left_bottom)
+
+    last_down = send_down(last_total)
+    first_down = send_down(first_total)
+    chip_sum = sum_chip(probe_total, last_down[1])
+    last_grad, last_over = finish(last_total, *(part + 0.0 * chip_sum for part in last_down))
+    first_grad, first_over = finish(first_total, *first_down)
+    waits = ((), (last_down[0],), (first_down[1],), (first_down[0],), last_over, ())
+    probe_grad = sum_everywhere(chip_sum, block, waits)
     return (jnp.stack([first_grad, last_grad]), probe_grad)
 
 

time: 199 us -> 196 us (0.985)
  the two profiles are of different devices: /device:TPU:57 before, /device:TPU:34 now
where the time goes in v3:
time: 196 us; the launch traced here: 194 us
  starting transfers between devices  107 us (55%)
  waiting for transfers between devices  55.9 us (29%)
  Pallas kernels  18.7 us (10%)
  other arithmetic  5.97 us (3%)
  local copies, waits for them, and re-layouts  4.75 us (2%)
  between operations  1.97 us (1%)
    ppermute x15, starting transfers between devices, exchange(): lax.ppermute(value, axis, [(i, i ^ bit) for i in range(lax.axis_size(axis...  54.8 us
    ppermute x4, waiting for transfers between devices, around(): lax.ppermute(value, 'col', [(i, i // 4 * 4 + (i + steps) % 4) for i in ra...  35.2 us
    ppermute x8, starting transfers between devices, from_behind(): lax.ppermute(value, axis, [(source, source + steps) for source in range(l...  32.7 us
    ppermute x15, waiting for transfers between devices, exchange(): lax.ppermute(value, axis, [(i, i ^ bit) for i in range(lax.axis_size(axis...  19.1 us
    pallas_call x3, Pallas kernels, call(): pl.pallas_call(body, grid=(capacity,), in_specs=[pl.BlockSpec(memory_spac...  15.3 us
    ppermute x4, starting transfers between devices, across(): passed = lax.ppermute(value, 'col', pairs)  11.2 us
    ppermute x4, starting transfers between devices, between(): return lax.ppermute(value, ('row', 'col'), pairs)  4.24 us
    ppermute x4, starting transfers between devices, around(): lax.ppermute(value, 'col', [(i, i // 4 * 4 + (i + steps) % 4) for i in ra...  4.16 us
  transfers between devices with their start and end apart: 35, of which 8 were waited for; matrix products, arithmetic and copies ran while one was open for 4% of the time, Pallas kernels for 7%

profile of v3, /device:TPU:34, one launch (start us, length us, event | category | flops | bytes accessed | tf_op | source)
XLA Modules:
  0.0 194.4 jit_solution(7460199981664286448)
XLA Ops:
  0.7 2.7 %fusion.11 = (f32[1,2,256,256]{3,2,1,0:T(8,128)S(1)}, f32[1,2,256,256]{3,2,1,0:T(8,128)S(1)}, f32[1,2,256,256]{3,2,1,0:T(8,128)}, f32[1,2,256,256]{3,2,1,0:T(8,128)}) fusion(f32[2,2,512,256]{3,2,1,0:T(8,128)} %own.5), kind=kLoop, calls=%fused_computation.60 | loop fusion | bytes 4194304 | tf_op jit(solution)/shard_map/slice | solution.py:369
  3.4 3.0 %collective-permute-start.1 = (f32[1,2,256,256]{3,2,1,0:T(8,128)S(1)}, f32[1,2,256,256]{3,2,1,0:T(8,128)}, u32[]{:S(2)}, u32[]{:S(2)}) collective-permute-start(f32[1,2,256,256]{3,2,1,0:T(8,128)S(1)} %get-tuple-element.17), channel_id=1, source_target_pairs={{0,3},{1,0},{2,1},{3,2},{4,7},{5,4},{6,5},{7,6},{8,11},{9,8},{10,9... | collective-permute-start | bytes 1572872 | tf_op jit(solution)/shard_map/ppermute | solution.py:280
  6.4 2.2 %collective-permute-start = (f32[1,2,256,256]{3,2,1,0:T(8,128)}, f32[1,2,256,256]{3,2,1,0:T(8,128)S(1)}, u32[]{:S(2)}, u32[]{:S(2)}) collective-permute-start(f32[1,2,256,256]{3,2,1,0:T(8,128)} %get-tuple-element.20), channel_id=1, source_target_pairs={{1,0},{2,1},{3,2},{4,3},{5,4},{6,5},{7,6},{8,7},{9,8},{10,9},{11,1... | collective-permute-start | bytes 1572872 | tf_op jit(solution)/shard_map/ppermute | solution.py:275
  8.6 1.0 collective-permute-start.7
  9.6 1.3 collective-permute-start.3
  10.9 1.9 collective-permute-start.6
  12.8 28.4 %collective-permute-done.1 = f32[1,2,256,256]{3,2,1,0:T(8,128)} collective-permute-done((f32[1,2,256,256]{3,2,1,0:T(8,128)S(1)}, f32[1,2,256,256]{3,2,1,0:T(8,128)}, u32[]{:S(2)}, u32[]{:S(2)}) %collective-permute-start.1) | collective-permute-done | bytes 524320 | tf_op jit(solution)/shard_map/ppermute | solution.py:280
  41.2 1.3 collective-permute-start.9
  42.5 1.5 collective-permute-start.2
  44.0 0.7 reorder.2
  44.7 6.7 %collective-permute-done.7 = f32[1,2,256,256]{3,2,1,0:T(8,128)} collective-permute-done((f32[1,2,256,256]{3,2,1,0:T(8,128)S(1)}, f32[1,2,256,256]{3,2,1,0:T(8,128)}, u32[]{:S(2)}, u32[]{:S(2)}) %collective-permute-start.7) | collective-permute-done | bytes 524320 | tf_op jit(solution)/shard_map/ppermute | solution.py:280
  51.3 1.5 collective-permute-start.8
  52.8 1.6 fusion.12
  55.2 2.7 %reorder.3.measured = f32[4,256,256]{2,1,0:T(8,128)S(1)} custom-call(f32[4,256,256]{2,1,0:T(8,128)S(1)} %bitcast.71, bf16[2,256,256]{2,1,0:T(8,128)(2,1)S(1)} %copy-done.2), custom_call_target="tpu_custom_call" | custom-call | flops 805306368 | bytes 2097152 | tf_op jit(solution)/shard_map/reorder/pallas_call | solution.py:103
  58.0 1.6 collective-permute-start.4
  59.6 0.7 collective-permute-start.5
  60.3 1.3 collective-permute-start.10
  61.6 0.7 collective-permute-start.11
  62.3 1.1 select_bitcast_fusion.1.right_bottom
  63.5 1.1 select_bitcast_fusion.right_bottom
  64.7 4.5 %arrive.1.arriving = f32[4,2,256,256]{3,2,1,0:T(8,128)S(1)} custom-call(s32[1,1]{1,0:T(1,128)S(6)} %copy.14.count, s32[4,2]{1,0:T(4,128)S(1)} %copy.13.offsets, f32[2,2,512,256]{3,2,1,0:T(8,128)S(1)} %copy-done, f32[2,256,256]{2,1,0:T(8,128)S(1)} %bitcast.72, f32[2,256,256]{2,1,0:T(8,128)S(1)} %select_bitcast_fusion.1.right_bottom, ...), custom_call_target="tpu_custom_call" | custom-call | flops 3221225472 | bytes 8388608 | tf_op jit(solution)/shard_map/arrive/pallas_call | solution.py:249
  69.2 1.6 collective-permute-done.10
  70.9 5.1 %misfit.1 = (f32[3,2,2,256,256]{4,3,2,1,0:T(8,128)S(1)}, f32[4,2,256,256]{3,2,1,0:T(8,128)S(1)}) custom-call(s32[1,1]{1,0:T(1,128)S(6)} %copy.14.count, s32[4,2]{1,0:T(4,128)S(1)} %copy.13.offsets, f32[2,2,512,256]{3,2,1,0:T(8,128)S(1)} %copy-done, f32[2,256,256]{2,1,0:T(8,128)S(1)} %bitcast.76, f32[2,256,256]{2,1,0:T(8,128)S(1)} %select_bitcast_fusion.right_bottom, ...), custom_call_target="tpu_custom_call" | custom-call | flops 3221225472 | bytes 8388608 | tf_op jit(solution)/shard_map/misfit/pallas_call | solution.py:249
  76.3 18.0 %collective-permute-start.16 = (f32[2,2,256,256]{3,2,1,0:T(8,128)S(1)}, f32[2,2,256,256]{3,2,1,0:T(8,128)S(1)}, u32[]{:S(2)}, u32[]{:S(2)}) collective-permute-start(f32[2,2,256,256]{3,2,1,0:T(8,128)S(1)} %slice_bitcast_fusion), channel_id=1, source_target_pairs={{0,32},{32,64},{64,96},{96,128},{128,160},{160,192},{192,224},{1,3... | collective-permute-start | bytes 3145736 | tf_op jit(solution)/shard_map/ppermute | solution.py:275
  94.3 5.7 %leave.1 = (f32[3,2,2,256,256]{4,3,2,1,0:T(8,128)S(1)}, f32[2,256,256]{2,1,0:T(8,128)S(1)}) custom-call(s32[1,1]{1,0:T(1,128)S(6)} %copy.14.count, s32[4,2]{1,0:T(4,128)S(1)} %copy.13.offsets, f32[2,2,512,256]{3,2,1,0:T(8,128)S(1)} %copy-done, f32[2,256,256]{2,1,0:T(8,128)S(1)} %bitcast.73, f32[2,256,256]{2,1,0:T(8,128)S(1)} %select_bitcast_fusion.1.right_bottom, ...), custom_call_target="tpu_custom_call" | custom-call | flops 25769803776 | bytes 8388608 | tf_op jit(solution)/shard_map/leave/pallas_call | solution.py:249
  100.3 5.0 %collective-permute-start.18 = (f32[256,256]{1,0:T(8,128)S(1)}, f32[256,256]{1,0:T(8,128)S(1)}, u32[]{:S(2)}, u32[]{:S(2)}) collective-permute-start(f32[256,256]{1,0:T(8,128)S(1)} %select_bitcast_fusion.2), channel_id=1, source_target_pairs={{0,32},{32,0},{64,96},{96,64},{128,160},{160,128},{192,224},{224,1... | collective-permute-start | bytes 786440 | tf_op jit(solution)/shard_map/ppermute | solution.py:299
  105.3 2.0 %collective-permute-start.12 = (f32[2,2,256,256]{3,2,1,0:T(8,128)S(1)}, f32[2,2,256,256]{3,2,1,0:T(8,128)S(1)}, u32[]{:S(2)}, u32[]{:S(2)}) collective-permute-start(f32[2,2,256,256]{3,2,1,0:T(8,128)S(1)} %slice_bitcast_fusion.1), channel_id=1, source_target_pairs={{0,32},{32,64},{64,96},{96,128},{128,160},{160,192},{192,224},{1,3... | collective-permute-start | bytes 3145736 | tf_op jit(solution)/shard_map/ppermute | solution.py:275
  107.4 2.9 %collective-permute-start.21 = (f32[64,256]{1,0:T(8,128)S(1)}, f32[64,256]{1,0:T(8,128)S(1)}, u32[]{:S(2)}, u32[]{:S(2)}) collective-permute-start(f32[64,256]{1,0:T(8,128)S(1)} %get-tuple-element.27), channel_id=1, source_target_pairs={{0,8},{1,9},{2,10},{3,11},{4,12},{5,13},{6,14},{7,15},{8,0},{9,1},... | collective-permute-start | bytes 196616 | tf_op jit(solution)/shard_map/ppermute | solution.py:299
  110.4 0.3 collective-permute-start.22
  110.7 1.3 collective-permute-start.23
  112.3 4.1 %collective-permute-start.19 = (f32[2,256,256]{2,1,0:T(8,128)S(1)}, f32[2,256,256]{2,1,0:T(8,128)S(1)}, u32[]{:S(2)}, u32[]{:S(2)}) collective-permute-start(f32[2,256,256]{2,1,0:T(8,128)S(1)} %fusion), channel_id=1, source_target_pairs={{0,1},{1,2},{2,3},{3,4},{4,5},{5,6},{6,7},{7,8},{8,9},{9,10},{10,1... | collective-permute-start | bytes 1572872 | tf_op jit(solution)/shard_map/ppermute | solution.py:275
  116.5 4.4 %collective-permute-start.20 = (f32[2,256,256]{2,1,0:T(8,128)S(1)}, f32[2,256,256]{2,1,0:T(8,128)S(1)}, u32[]{:S(2)}, u32[]{:S(2)}) collective-permute-start(f32[2,256,256]{2,1,0:T(8,128)S(1)} %broadcast_add_fusion.1), channel_id=1, source_target_pairs={{0,4},{4,8},{8,12},{12,16},{16,20},{20,24},{24,28},{32,36},{36,40}... | collective-permute-start | bytes 1572872 | tf_op jit(solution)/shard_map/ppermute | solution.py:287
  121.1 2.9 %collective-permute-start.25 = (f32[64,256]{1,0:T(8,128)S(1)}, f32[64,256]{1,0:T(8,128)S(1)}, u32[]{:S(2)}, u32[]{:S(2)}) collective-permute-start(f32[64,256]{1,0:T(8,128)S(1)} %fusion.10), channel_id=1, source_target_pairs={{0,2},{1,3},{2,0},{3,1},{4,6},{5,7},{6,4},{7,5},{8,10},{9,11},{10,... | collective-permute-start | bytes 196616 | tf_op jit(solution)/shard_map/ppermute | solution.py:299
  124.0 1.8 collective-permute-start.26
  125.8 3.8 %collective-permute-start.15 = (f32[2,256,256]{2,1,0:T(8,128)S(1)}, f32[2,256,256]{2,1,0:T(8,128)S(1)}, u32[]{:S(2)}, u32[]{:S(2)}) collective-permute-start(f32[2,256,256]{2,1,0:T(8,128)S(1)} %collective-permute-done.14), channel_id=1, source_target_pairs={{0,4},{4,8},{8,12},{12,16},{16,20},{20,24},{24,28},{32,36},{36,40}... | collective-permute-start | bytes 1572872 | tf_op jit(solution)/shard_map/ppermute | solution.py:287
  129.7 1.9 collective-permute-start.13
  131.7 25.4 %collective-permute-start.27 = (f32[64,256]{1,0:T(8,128)S(1)}, f32[64,256]{1,0:T(8,128)S(1)}, u32[]{:S(2)}, u32[]{:S(2)}) collective-permute-start(f32[64,256]{1,0:T(8,128)S(1)} %fusion.9), channel_id=1, source_target_pairs={{0,64},{32,96},{64,0},{96,32},{128,192},{160,224},{192,128},{224,1... | collective-permute-start | bytes 196616 | tf_op jit(solution)/shard_map/ppermute | solution.py:299
  157.0 9.3 %collective-permute-start.28 = (f32[64,256]{1,0:T(8,128)S(1)}, f32[64,256]{1,0:T(8,128)S(1)}, u32[]{:S(2)}, u32[]{:S(2)}) collective-permute-start(f32[64,256]{1,0:T(8,128)S(1)} %fusion.9), channel_id=1, source_target_pairs={{0,128},{32,160},{64,192},{96,224},{128,0},{160,32},{192,64},{224,... | collective-permute-start | bytes 196616 | tf_op jit(solution)/shard_map/ppermute | solution.py:299
  166.3 0.2 bitcast_add_fusion
  166.6 10.8 %collective-permute-done.28 = f32[64,256]{1,0:T(8,128)S(1)} collective-permute-done((f32[64,256]{1,0:T(8,128)S(1)}, f32[64,256]{1,0:T(8,128)S(1)}, u32[]{:S(2)}, u32[]{:S(2)}) %collective-permute-start.28) | collective-permute-done | bytes 65568 | tf_op jit(solution)/shard_map/ppermute | solution.py:299
  177.5 0.2 fusion.5
  177.8 4.0 %collective-permute-done.30 = f32[64,256]{1,0:T(8,128)S(1)} collective-permute-done((f32[64,256]{1,0:T(8,128)S(1)}, f32[64,256]{1,0:T(8,128)S(1)}, u32[]{:S(2)}, u32[]{:S(2)}) %collective-permute-start.30) | collective-permute-done | bytes 65568 | tf_op jit(solution)/shard_map/ppermute | solution.py:299
  181.8 0.3 collective-permute-start.31
  182.1 5.4 %collective-permute-start.32 = (f32[64,256]{1,0:T(8,128)S(1)}, f32[64,256]{1,0:T(8,128)S(1)}, u32[]{:S(2)}, u32[]{:S(2)}) collective-permute-start(f32[64,256]{1,0:T(8,128)S(1)} %add.136), channel_id=1, source_target_pairs={{0,16},{1,17},{2,18},{3,19},{4,20},{5,21},{6,22},{7,23},{8,24},{9,... | collective-permute-start | bytes 196616 | tf_op jit(solution)/shard_map/ppermute | solution.py:299
  187.6 2.7 %collective-permute-done.32 = f32[64,256]{1,0:T(8,128)S(1)} collective-permute-done((f32[64,256]{1,0:T(8,128)S(1)}, f32[64,256]{1,0:T(8,128)S(1)}, u32[]{:S(2)}, u32[]{:S(2)}) %collective-permute-start.32) | collective-permute-done | bytes 65568 | tf_op jit(solution)/shard_map/ppermute | solution.py:299
  190.4 1.4 collective-permute-done.33
  192.0 1.5 pad_maximum_fusion
  193.6 0.8 pad_maximum_fusion.2
  (79 shorter events, 2.0 us)
Async XLA Ops:
  0.6 43.4 %copy-start.2 = (bf16[2,256,256]{2,1,0:T(8,128)(2,1)S(1)}, bf16[2,256,256]{2,1,0:T(8,128)(2,1)}, u32[]{:S(2)}) copy-start(bf16[2,256,256]{2,1,0:T(8,128)(2,1)} %constant.44.clone.pick) | copy-start | bytes 786436
  0.6 43.3 %copy-start.1 = (f32[256,256]{1,0:T(8,128)S(1)}, f32[256,256]{1,0:T(8,128)}, u32[]{:S(2)}) copy-start(f32[256,256]{1,0:T(8,128)} %param.11) | copy-start | bytes 786436
  0.7 53.8 %copy-start.8 = (s32[1,1,4,2]{2,3,1,0:T(2,128)S(1)}, s32[1,1,4,2]{2,3,1,0:T(2,128)}, u32[]{:S(2)}) copy-start(s32[1,1,4,2]{2,3,1,0:T(2,128)} %param.13) | copy-start | bytes 100
  0.7 54.5 %copy-start.3 = (f32[1,1,4,256,256]{4,3,2,1,0:T(8,128)S(1)}, f32[1,1,4,256,256]{4,3,2,1,0:T(8,128)}, u32[]{:S(2)}) copy-start(f32[1,1,4,256,256]{4,3,2,1,0:T(8,128)} %param.14) | copy-start | bytes 3145732
  3.4 37.8 %collective-permute-start.1 = (f32[1,2,256,256]{3,2,1,0:T(8,128)S(1)}, f32[1,2,256,256]{3,2,1,0:T(8,128)}, u32[]{:S(2)}, u32[]{:S(2)}) collective-permute-start(f32[1,2,256,256]{3,2,1,0:T(8,128)S(1)} %get-tuple-element.17), channel_id=1, source_target_pairs={{0,3},{1,0},{2,1},{3,2},{4,7},{5,4},{6,5},{7,6},{8,11},{9,8},{10,9... | collective-permute-start | bytes 1572872 | tf_op jit(solution)/shard_map/ppermute | solution.py:280
  6.4 36.1 %collective-permute-start = (f32[1,2,256,256]{3,2,1,0:T(8,128)}, f32[1,2,256,256]{3,2,1,0:T(8,128)S(1)}, u32[]{:S(2)}, u32[]{:S(2)}) collective-permute-start(f32[1,2,256,256]{3,2,1,0:T(8,128)} %get-tuple-element.20), channel_id=1, source_target_pairs={{1,0},{2,1},{3,2},{4,3},{5,4},{6,5},{7,6},{8,7},{9,8},{10,9},{11,1... | collective-permute-start | bytes 1572872 | tf_op jit(solution)/shard_map/ppermute | solution.py:275
  8.6 42.7 %collective-permute-start.7 = (f32[1,2,256,256]{3,2,1,0:T(8,128)S(1)}, f32[1,2,256,256]{3,2,1,0:T(8,128)}, u32[]{:S(2)}, u32[]{:S(2)}) collective-permute-start(f32[1,2,256,256]{3,2,1,0:T(8,128)S(1)} %get-tuple-element.18), channel_id=1, source_target_pairs={{0,3},{1,0},{2,1},{3,2},{4,7},{5,4},{6,5},{7,6},{8,11},{9,8},{10,9... | collective-permute-start | bytes 1572872 | tf_op jit(solution)/shard_map/ppermute | solution.py:280
  9.6 48.4 %collective-permute-start.3 = (f32[1,2,256,256]{3,2,1,0:T(8,128)}, f32[1,2,256,256]{3,2,1,0:T(8,128)S(1)}, u32[]{:S(2)}, u32[]{:S(2)}) collective-permute-start(f32[1,2,256,256]{3,2,1,0:T(8,128)} %get-tuple-element.20), channel_id=1, source_target_pairs={{32,0},{64,32},{96,64},{128,96},{160,128},{192,160},{224,192},{33,... | collective-permute-start | bytes 1572872 | tf_op jit(solution)/shard_map/ppermute | solution.py:275
  10.9 48.7 %collective-permute-start.6 = (f32[1,2,256,256]{3,2,1,0:T(8,128)}, f32[1,2,256,256]{3,2,1,0:T(8,128)S(1)}, u32[]{:S(2)}, u32[]{:S(2)}) collective-permute-start(f32[1,2,256,256]{3,2,1,0:T(8,128)} %get-tuple-element.19), channel_id=1, source_target_pairs={{1,0},{2,1},{3,2},{4,3},{5,4},{6,5},{7,6},{8,7},{9,8},{10,9},{11,1... | collective-permute-start | bytes 1572872 | tf_op jit(solution)/shard_map/ppermute | solution.py:275
  41.2 19.1 %collective-permute-start.9 = (f32[1,2,256,256]{3,2,1,0:T(8,128)}, f32[1,2,256,256]{3,2,1,0:T(8,128)S(1)}, u32[]{:S(2)}, u32[]{:S(2)}) collective-permute-start(f32[1,2,256,256]{3,2,1,0:T(8,128)} %get-tuple-element.19), channel_id=1, source_target_pairs={{32,0},{64,32},{96,64},{128,96},{160,128},{192,160},{224,192},{33,... | collective-permute-start | bytes 1572872 | tf_op jit(solution)/shard_map/ppermute | solution.py:275
  42.5 19.1 %collective-permute-start.2 = (f32[1,2,256,256]{3,2,1,0:T(8,128)}, f32[1,2,256,256]{3,2,1,0:T(8,128)}, u32[]{:S(2)}, u32[]{:S(2)}) collective-permute-start(f32[1,2,256,256]{3,2,1,0:T(8,128)} %collective-permute-done.1), channel_id=1, source_target_pairs={{7,3},{11,7},{15,11},{19,15},{23,19},{27,23},{31,27},{39,35},{43,3... | collective-permute-start | bytes 1572872 | tf_op jit(solution)/shard_map/ppermute | solution.py:287
  51.3 12.2 %collective-permute-start.8 = (f32[1,2,256,256]{3,2,1,0:T(8,128)}, f32[1,2,256,256]{3,2,1,0:T(8,128)}, u32[]{:S(2)}, u32[]{:S(2)}) collective-permute-start(f32[1,2,256,256]{3,2,1,0:T(8,128)} %collective-permute-done.7), channel_id=1, source_target_pairs={{7,3},{11,7},{15,11},{19,15},{23,19},{27,23},{31,27},{39,35},{43,3... | collective-permute-start | bytes 1572872 | tf_op jit(solution)/shard_map/ppermute | solution.py:287
  55.2 2.8 %copy-start.6 = (f32[1,256,256]{2,1,0:T(8,128)S(1)}, f32[1,256,256]{2,1,0:T(8,128)}, u32[]{:S(2)}) copy-start(f32[1,256,256]{2,1,0:T(8,128)} %get-tuple-element.30) | copy-start | bytes 786436
  55.2 2.8 %copy-start.7 = (f32[1,256,256]{2,1,0:T(8,128)S(1)}, f32[1,256,256]{2,1,0:T(8,128)}, u32[]{:S(2)}) copy-start(f32[1,256,256]{2,1,0:T(8,128)} %get-tuple-element.31) | copy-start | bytes 786436
  57.9 6.8 %copy-start = (f32[2,2,512,256]{3,2,1,0:T(8,128)S(1)}, f32[2,2,512,256]{3,2,1,0:T(8,128)}, u32[]{:S(2)}) copy-start(f32[2,2,512,256]{3,2,1,0:T(8,128)} %own.5) | copy-start | bytes 6291460
  57.9 6.8 %copy-start.4 = (f32[2,256,256]{2,1,0:T(8,128)S(1)}, f32[2,256,256]{2,1,0:T(8,128)}, u32[]{:S(2)}) copy-start(f32[2,256,256]{2,1,0:T(8,128)} %probe.3) | copy-start | bytes 1572868
  58.0 6.8 %copy-start.5 = (bf16[2,2,2,256,256]{4,3,2,1,0:T(8,128)(2,1)S(1)}, bf16[2,2,2,256,256]{4,3,2,1,0:T(8,128)(2,1)}, u32[]{:S(2)}) copy-start(bf16[2,2,2,256,256]{4,3,2,1,0:T(8,128)(2,1)} %constant.45.clone.tables) | copy-start | bytes 3145732
  58.0 6.6 %collective-permute-start.4 = (f32[1,2,256,256]{3,2,1,0:T(8,128)S(1)}, f32[1,2,256,256]{3,2,1,0:T(8,128)S(1)}, u32[]{:S(2)}, u32[]{:S(2)}) collective-permute-start(f32[1,2,256,256]{3,2,1,0:T(8,128)S(1)} %collective-permute-done), channel_id=1, source_target_pairs={{32,0},{33,1},{34,2},{35,3},{36,4},{37,5},{38,6},{39,7},{40,8},{41... | collective-permute-start | bytes 1572872 | tf_op jit(solution)/shard_map/ppermute | solution.py:366
  59.6 5.0 %collective-permute-start.5 = (f32[1,2,256,256]{3,2,1,0:T(8,128)S(1)}, f32[1,2,256,256]{3,2,1,0:T(8,128)S(1)}, u32[]{:S(2)}, u32[]{:S(2)}) collective-permute-start(f32[1,2,256,256]{3,2,1,0:T(8,128)S(1)} %collective-permute-done.3), channel_id=1, source_target_pairs={{33,32},{34,33},{35,34},{36,35},{37,36},{38,37},{39,38},{40,39},{4... | collective-permute-start | bytes 1572872 | tf_op jit(solution)/shard_map/ppermute | solution.py:366
  60.3 10.5 %collective-permute-start.10 = (f32[1,2,256,256]{3,2,1,0:T(8,128)S(1)}, f32[1,2,256,256]{3,2,1,0:T(8,128)S(1)}, u32[]{:S(2)}, u32[]{:S(2)}) collective-permute-start(f32[1,2,256,256]{3,2,1,0:T(8,128)S(1)} %collective-permute-done.6), channel_id=1, source_target_pairs={{32,0},{33,1},{34,2},{35,3},{36,4},{37,5},{38,6},{39,7},{40,8},{41... | collective-permute-start | bytes 1572872 | tf_op jit(solution)/shard_map/ppermute | solution.py:366
  61.6 9.2 %collective-permute-start.11 = (f32[1,2,256,256]{3,2,1,0:T(8,128)S(1)}, f32[1,2,256,256]{3,2,1,0:T(8,128)S(1)}, u32[]{:S(2)}, u32[]{:S(2)}) collective-permute-start(f32[1,2,256,256]{3,2,1,0:T(8,128)S(1)} %collective-permute-done.9), channel_id=1, source_target_pairs={{33,32},{34,33},{35,34},{36,35},{37,36},{38,37},{39,38},{40,39},{4... | collective-permute-start | bytes 1572872 | tf_op jit(solution)/shard_map/ppermute | solution.py:366
  76.2 24.0 %collective-permute-start.17 = (f32[2,256,256]{2,1,0:T(8,128)S(1)}, f32[2,256,256]{2,1,0:T(8,128)S(1)}, u32[]{:S(2)}, u32[]{:S(2)}) collective-permute-start(f32[2,256,256]{2,1,0:T(8,128)S(1)} %slice_bitcast_fusion.6), channel_id=1, source_target_pairs={{0,1},{1,2},{2,3},{3,0},{4,5},{5,6},{6,7},{7,4},{8,9},{9,10},{10,1... | collective-permute-start | bytes 1572872 | tf_op jit(solution)/shard_map/ppermute | solution.py:280
  76.3 31.1 %collective-permute-start.16 = (f32[2,2,256,256]{3,2,1,0:T(8,128)S(1)}, f32[2,2,256,256]{3,2,1,0:T(8,128)S(1)}, u32[]{:S(2)}, u32[]{:S(2)}) collective-permute-start(f32[2,2,256,256]{3,2,1,0:T(8,128)S(1)} %slice_bitcast_fusion), channel_id=1, source_target_pairs={{0,32},{32,64},{64,96},{96,128},{128,160},{160,192},{192,224},{1,3... | collective-permute-start | bytes 3145736 | tf_op jit(solution)/shard_map/ppermute | solution.py:275
  100.1 12.3 %collective-permute-start.14 = (f32[2,256,256]{2,1,0:T(8,128)S(1)}, f32[2,256,256]{2,1,0:T(8,128)S(1)}, u32[]{:S(2)}, u32[]{:S(2)}) collective-permute-start(f32[2,256,256]{2,1,0:T(8,128)S(1)} %slice_bitcast_fusion.7), channel_id=1, source_target_pairs={{0,1},{1,2},{2,3},{3,0},{4,5},{5,6},{6,7},{7,4},{8,9},{9,10},{10,1... | collective-permute-start | bytes 1572872 | tf_op jit(solution)/shard_map/ppermute | solution.py:280
  100.3 7.0 %collective-permute-start.18 = (f32[256,256]{1,0:T(8,128)S(1)}, f32[256,256]{1,0:T(8,128)S(1)}, u32[]{:S(2)}, u32[]{:S(2)}) collective-permute-start(f32[256,256]{1,0:T(8,128)S(1)} %select_bitcast_fusion.2), channel_id=1, source_target_pairs={{0,32},{32,0},{64,96},{96,64},{128,160},{160,128},{192,224},{224,1... | collective-permute-start | bytes 786440 | tf_op jit(solution)/shard_map/ppermute | solution.py:299
  105.3 18.6 %collective-permute-start.12 = (f32[2,2,256,256]{3,2,1,0:T(8,128)S(1)}, f32[2,2,256,256]{3,2,1,0:T(8,128)S(1)}, u32[]{:S(2)}, u32[]{:S(2)}) collective-permute-start(f32[2,2,256,256]{3,2,1,0:T(8,128)S(1)} %slice_bitcast_fusion.1), channel_id=1, source_target_pairs={{0,32},{32,64},{64,96},{96,128},{128,160},{160,192},{192,224},{1,3... | collective-permute-start | bytes 3145736 | tf_op jit(solution)/shard_map/ppermute | solution.py:275
  107.4 9.0 %collective-permute-start.21 = (f32[64,256]{1,0:T(8,128)S(1)}, f32[64,256]{1,0:T(8,128)S(1)}, u32[]{:S(2)}, u32[]{:S(2)}) collective-permute-start(f32[64,256]{1,0:T(8,128)S(1)} %get-tuple-element.27), channel_id=1, source_target_pairs={{0,8},{1,9},{2,10},{3,11},{4,12},{5,13},{6,14},{7,15},{8,0},{9,1},... | collective-permute-start | bytes 196616 | tf_op jit(solution)/shard_map/ppermute | solution.py:299
  110.4 10.5 %collective-permute-start.22 = (f32[64,256]{1,0:T(8,128)S(1)}, f32[64,256]{1,0:T(8,128)S(1)}, u32[]{:S(2)}, u32[]{:S(2)}) collective-permute-start(f32[64,256]{1,0:T(8,128)S(1)} %get-tuple-element.28), channel_id=1, source_target_pairs={{0,16},{1,17},{2,18},{3,19},{4,20},{5,21},{6,22},{7,23},{8,24},{9,... | collective-permute-start | bytes 196616 | tf_op jit(solution)/shard_map/ppermute | solution.py:299
  110.7 10.2 %collective-permute-start.23 = (f32[64,256]{1,0:T(8,128)S(1)}, f32[64,256]{1,0:T(8,128)S(1)}, u32[]{:S(2)}, u32[]{:S(2)}) collective-permute-start(f32[64,256]{1,0:T(8,128)S(1)} %get-tuple-element.29), channel_id=1, source_target_pairs={{0,24},{1,25},{2,26},{3,27},{4,28},{5,29},{6,30},{7,31},{8,16},{9,... | collective-permute-start | bytes 196616 | tf_op jit(solution)/shard_map/ppermute | solution.py:299
  112.3 44.7 %collective-permute-start.19 = (f32[2,256,256]{2,1,0:T(8,128)S(1)}, f32[2,256,256]{2,1,0:T(8,128)S(1)}, u32[]{:S(2)}, u32[]{:S(2)}) collective-permute-start(f32[2,256,256]{2,1,0:T(8,128)S(1)} %fusion), channel_id=1, source_target_pairs={{0,1},{1,2},{2,3},{3,4},{4,5},{5,6},{6,7},{7,8},{8,9},{9,10},{10,1... | collective-permute-start | bytes 1572872 | tf_op jit(solution)/shard_map/ppermute | solution.py:275
  116.5 49.8 %collective-permute-start.20 = (f32[2,256,256]{2,1,0:T(8,128)S(1)}, f32[2,256,256]{2,1,0:T(8,128)S(1)}, u32[]{:S(2)}, u32[]{:S(2)}) collective-permute-start(f32[2,256,256]{2,1,0:T(8,128)S(1)} %broadcast_add_fusion.1), channel_id=1, source_target_pairs={{0,4},{4,8},{8,12},{12,16},{16,20},{20,24},{24,28},{32,36},{36,40}... | collective-permute-start | bytes 1572872 | tf_op jit(solution)/shard_map/ppermute | solution.py:287
  121.0 4.9 %collective-permute-start.24 = (f32[64,256]{1,0:T(8,128)S(1)}, f32[64,256]{1,0:T(8,128)S(1)}, u32[]{:S(2)}, u32[]{:S(2)}) collective-permute-start(f32[64,256]{1,0:T(8,128)S(1)} %fusion.10), channel_id=1, source_target_pairs={{0,1},{1,0},{2,3},{3,2},{4,5},{5,4},{6,7},{7,6},{8,9},{9,8},{10,11... | collective-permute-start | bytes 196616 | tf_op jit(solution)/shard_map/ppermute | solution.py:299
  121.1 8.6 %collective-permute-start.25 = (f32[64,256]{1,0:T(8,128)S(1)}, f32[64,256]{1,0:T(8,128)S(1)}, u32[]{:S(2)}, u32[]{:S(2)}) collective-permute-start(f32[64,256]{1,0:T(8,128)S(1)} %fusion.10), channel_id=1, source_target_pairs={{0,2},{1,3},{2,0},{3,1},{4,6},{5,7},{6,4},{7,5},{8,10},{9,11},{10,... | collective-permute-start | bytes 196616 | tf_op jit(solution)/shard_map/ppermute | solution.py:299
  124.0 7.7 %collective-permute-start.26 = (f32[64,256]{1,0:T(8,128)S(1)}, f32[64,256]{1,0:T(8,128)S(1)}, u32[]{:S(2)}, u32[]{:S(2)}) collective-permute-start(f32[64,256]{1,0:T(8,128)S(1)} %fusion.10), channel_id=1, source_target_pairs={{0,3},{1,2},{2,1},{3,0},{4,7},{5,6},{6,5},{7,4},{8,11},{9,10},{10,... | collective-permute-start | bytes 196616 | tf_op jit(solution)/shard_map/ppermute | solution.py:299
  125.8 51.7 %collective-permute-start.15 = (f32[2,256,256]{2,1,0:T(8,128)S(1)}, f32[2,256,256]{2,1,0:T(8,128)S(1)}, u32[]{:S(2)}, u32[]{:S(2)}) collective-permute-start(f32[2,256,256]{2,1,0:T(8,128)S(1)} %collective-permute-done.14), channel_id=1, source_target_pairs={{0,4},{4,8},{8,12},{12,16},{16,20},{20,24},{24,28},{32,36},{36,40}... | collective-permute-start | bytes 1572872 | tf_op jit(solution)/shard_map/ppermute | solution.py:287
  129.7 47.8 %collective-permute-start.13 = (f32[2,256,256]{2,1,0:T(8,128)S(1)}, f32[2,256,256]{2,1,0:T(8,128)S(1)}, u32[]{:S(2)}, u32[]{:S(2)}) collective-permute-start(f32[2,256,256]{2,1,0:T(8,128)S(1)} %fusion.3), channel_id=1, source_target_pairs={{0,1},{1,2},{2,3},{3,4},{4,5},{5,6},{6,7},{7,8},{8,9},{9,10},{10,1... | collective-permute-start | bytes 1572872 | tf_op jit(solution)/shard_map/ppermute | solution.py:275
  131.7 34.9 %collective-permute-start.27 = (f32[64,256]{1,0:T(8,128)S(1)}, f32[64,256]{1,0:T(8,128)S(1)}, u32[]{:S(2)}, u32[]{:S(2)}) collective-permute-start(f32[64,256]{1,0:T(8,128)S(1)} %fusion.9), channel_id=1, source_target_pairs={{0,64},{32,96},{64,0},{96,32},{128,192},{160,224},{192,128},{224,1... | collective-permute-start | bytes 196616 | tf_op jit(solution)/shard_map/ppermute | solution.py:299
  157.0 20.4 %collective-permute-start.28 = (f32[64,256]{1,0:T(8,128)S(1)}, f32[64,256]{1,0:T(8,128)S(1)}, u32[]{:S(2)}, u32[]{:S(2)}) collective-permute-start(f32[64,256]{1,0:T(8,128)S(1)} %fusion.9), channel_id=1, source_target_pairs={{0,128},{32,160},{64,192},{96,224},{128,0},{160,32},{192,64},{224,... | collective-permute-start | bytes 196616 | tf_op jit(solution)/shard_map/ppermute | solution.py:299
  166.3 11.1 %collective-permute-start.29 = (f32[64,256]{1,0:T(8,128)S(1)}, f32[64,256]{1,0:T(8,128)S(1)}, u32[]{:S(2)}, u32[]{:S(2)}) collective-permute-start(f32[64,256]{1,0:T(8,128)S(1)} %fusion.9), channel_id=1, source_target_pairs={{0,192},{32,224},{64,128},{96,160},{128,64},{160,96},{192,0},{224,... | collective-permute-start | bytes 196616 | tf_op jit(solution)/shard_map/ppermute | solution.py:299
  177.4 4.4 %collective-permute-start.30 = (f32[64,256]{1,0:T(8,128)S(1)}, f32[64,256]{1,0:T(8,128)S(1)}, u32[]{:S(2)}, u32[]{:S(2)}) collective-permute-start(f32[64,256]{1,0:T(8,128)S(1)} %fusion.7), channel_id=1, source_target_pairs={{0,4},{1,5},{2,6},{3,7},{4,0},{5,1},{6,2},{7,3},{8,12},{9,13},{10,... | collective-permute-start | bytes 196616 | tf_op jit(solution)/shard_map/ppermute | solution.py:299
  181.8 5.8 %collective-permute-start.31 = (f32[64,256]{1,0:T(8,128)S(1)}, f32[64,256]{1,0:T(8,128)S(1)}, u32[]{:S(2)}, u32[]{:S(2)}) collective-permute-start(f32[64,256]{1,0:T(8,128)S(1)} %add.136), channel_id=1, source_target_pairs={{0,24},{1,25},{2,26},{3,27},{4,28},{5,29},{6,30},{7,31},{8,16},{9,... | collective-permute-start | bytes 196616 | tf_op jit(solution)/shard_map/ppermute | solution.py:299
  182.1 8.3 %collective-permute-start.32 = (f32[64,256]{1,0:T(8,128)S(1)}, f32[64,256]{1,0:T(8,128)S(1)}, u32[]{:S(2)}, u32[]{:S(2)}) collective-permute-start(f32[64,256]{1,0:T(8,128)S(1)} %add.136), channel_id=1, source_target_pairs={{0,16},{1,17},{2,18},{3,19},{4,20},{5,21},{6,22},{7,23},{8,24},{9,... | collective-permute-start | bytes 196616 | tf_op jit(solution)/shard_map/ppermute | solution.py:299
  187.5 4.3 %collective-permute-start.33 = (f32[64,256]{1,0:T(8,128)S(1)}, f32[64,256]{1,0:T(8,128)S(1)}, u32[]{:S(2)}, u32[]{:S(2)}) collective-permute-start(f32[64,256]{1,0:T(8,128)S(1)} %add.136), channel_id=1, source_target_pairs={{0,8},{1,9},{2,10},{3,11},{4,12},{5,13},{6,14},{7,15},{8,0},{9,1},... | collective-permute-start | bytes 196616 | tf_op jit(solution)/shard_map/ppermute | solution.py:299
  191.9 1.7 collective-permute-start.34
